TPU v7x, 32 devices: a whole 2x2x4 slice. The times are simulated.
32 devices in a mesh: slab: 16 (over z, x, core), grp: 2 (over y).
Axes of the slice: x: 2, y: 2, z: 4, core: 2. Of those that a mesh axis runs over, the one named last changes fastest.
Arguments:
- adj_out: float32 [5, 128, 64, 256], P(None, 'grp', 'slab'), may hold values from -6 to 6
- advect: bfloat16 [3, 128, 64, 256], P(None, 'grp', 'slab'), may hold values from -4 to 4
- viscosity: bfloat16 [128, 64, 256], P('grp', 'slab'), may hold values from 0.099609375 to 0.796875
- body_mask: int32 [128, 64, 256], P('grp', 'slab'), may hold values 0 or 1
- marker_x: int32 [2048], replicated, may hold values from 32 to 47
- marker_z: int32 [2048], replicated, may hold values from 0 to 63
- marker_y: int32 [2048], replicated, may hold values from 64 to 191
- drag_weight: float32 [2048], replicated, may hold values from -5 to 5
- inv_x: float32 [128, 128], P(None, 'grp'), may hold values from 0 to 1, as said below
- inv_y: float32 [256, 256], replicated, may hold values from 0 to 1, as said below
- inv_z: float32 [64, 64], replicated, may hold values from 0 to 1, as said below
Outputs:
- state_adjoint: float32 [5, 128, 64, 256], P(None, 'grp', 'slab')
Inputs may be any that keep to these rules, and one draw needn't show every extreme that they name: `inv_x`: entries of a given inverse. `inv_y`: entries of a given inverse. `inv_z`: entries of a given inverse.
All inputs are finite; a program needn't handle non-finite values. No bound on the sum of `body_mask` on one device may be relied on, other than what follows from the above.
Results may differ from a plain program's by a relative error of at most 0.0003.
Values sent between devices are 32-bit elements; how exact they have to be, the bound alone decides.
A program may use at most 64 MiB of HBM per device.

v0:
```python
import jax
import jax.numpy as jnp
from jax import lax
from jax.sharding import PartitionSpec as P

time_step = 0.08
highest = lax.Precision.HIGHEST


def extended(cells, sides, width):
    for axis, dim in sides:
        count = lax.axis_size(axis)
        ends = count - 1
        head = lax.slice_in_dim(cells, 0, width, axis=dim)
        tail = lax.slice_in_dim(cells, cells.shape[dim] - width, cells.shape[dim], axis=dim)
        cells = jnp.concatenate(
            [
                lax.ppermute(tail, axis, [(i, (i + 1) % count) for i in range(ends)]),
                cells,
                lax.ppermute(head, axis, [((i + 1) % count, i) for i in range(ends)]),
            ],
            axis=dim,
        )
    return cells


def body(
    adj_out,
    advect,
    viscosity,
    body_mask,
    marker_x,
    marker_z,
    marker_y,
    drag_weight,
    inv_x,
    inv_y,
    inv_z,
):
    fields, x_rows, z_rows, y_cells = adj_out.shape
    x_offset = lax.axis_index("grp") * x_rows
    z_offset = lax.axis_index("slab") * z_rows
    local_x = marker_x - x_offset
    local_z = marker_z - z_offset
    inside = (local_x >= 0) & (local_x < x_rows) & (local_z >= 0) & (local_z < z_rows)
    flat_index = jnp.where(inside, (local_x * z_rows + local_z) * y_cells + marker_y, 0)
    pushed = jax.ops.segment_sum(
        jnp.where(inside, drag_weight, 0.0), flat_index, num_segments=x_rows * z_rows * y_cells
    )
    seeded = adj_out.at[0].add(pushed.reshape(x_rows, z_rows, y_cells))
    zlines = lax.all_to_all(seeded, "slab", split_axis=1, concat_axis=2, tiled=True)
    zlines = jnp.einsum("jk,cxjy->cxky", inv_z, zlines, precision=highest)
    zlines = jnp.einsum("jk,cxzj->cxzk", inv_y, zlines, precision=highest)
    returned = lax.all_to_all(zlines, "slab", split_axis=2, concat_axis=1, tiled=True)
    solved = jnp.einsum(
        "jk,cjzy->ckzy",
        inv_x,
        lax.all_gather(returned, "grp", axis=1, tiled=True),
        precision=highest,
    )
    masked = solved * body_mask.astype(jnp.float32)
    rimmed = extended(masked, (("slab", 2), ("grp", 1)), 1)
    centre = rimmed[:, 1:-1, 1:-1, :]
    y_padded = jnp.pad(centre, ((0, 0), (0, 0), (0, 0), (1, 1)))
    grad_x = (rimmed[:, 2:, 1:-1, :] - rimmed[:, :-2, 1:-1, :]) * 0.5
    grad_z = (rimmed[:, 1:-1, 2:, :] - rimmed[:, 1:-1, :-2, :]) * 0.5
    grad_y = (y_padded[..., 2:] - y_padded[..., :-2]) * 0.5
    laplace = (
        rimmed[:, 2:, 1:-1, :]
        + rimmed[:, :-2, 1:-1, :]
        + rimmed[:, 1:-1, 2:, :]
        + rimmed[:, 1:-1, :-2, :]
        + y_padded[..., 2:]
        + y_padded[..., :-2]
        - 6.0 * centre
    )
    velocity = advect.astype(jnp.float32)
    viscous = viscosity.astype(jnp.float32)
    change = velocity[0] * grad_x + velocity[1] * grad_z + velocity[2] * grad_y + viscous * laplace
    return centre + time_step * change


def solution(mesh):
    in_specs = (
        P(None, "grp", "slab", None),
        P(None, "grp", "slab", None),
        P("grp", "slab", None),
        P("grp", "slab", None),
        P(),
        P(),
        P(),
        P(),
        P(None, "grp"),
        P(),
        P(),
    )
    out_specs = P(None, "grp", "slab", None)
    return jax.shard_map(body, mesh=mesh, in_specs=in_specs, out_specs=out_specs, check_vma=False)
```

profile of v0, /device:TPU:1, one launch (start us, length us, event | category | flops | bytes accessed | tf_op | source)
XLA Modules:
  0.0 175.7 jit_solution(13865979738109163888)
XLA Ops:
  6.5 0.0 copy-start
  6.5 0.0 all-gather.2.cloned.1.call-start
  6.5 0.8 add_select_fusion
  7.3 0.7 broadcast_select_fusion
  8.1 14.0 %scatter_custom_fusion = f32[65536]{0:T(1024)S(1)} fusion(s32[2048]{0:T(1024)S(1)} %add_select_fusion, f32[2048]{0:T(1024)S(1)} %broadcast_select_fusion, f32[]{:T(128)} %constant.45.clone.1), kind=kCustom, calls=%fused_computation.27 | custom fusion | flops 2048 | bytes 262148 | tf_op jit(solution)/shard_map/scatter-add | solution.py:47
  22.0 0.1 reshape.47
  22.2 1.5 copy.28
  23.7 0.1 fusion.5
  23.8 39.0 %all_to_all.36 = f32[5,64,4,256]{3,2,0,1:T(4,128)S(1)} all-to-all(f32[5,64,4,256]{3,2,0,1:T(4,128)S(1)} %fusion.5), channel_id=1, replica_groups=mesh['slab'=16,'grp'=2] {'slab'}, dimensions={1} | all-to-all | bytes 2621440 | tf_op jit(solution)/shard_map/all_to_all | solution.py:51
  62.8 0.0 copy-start.5
  62.8 0.5 copy.29
  63.3 0.3 copy-done.5
  63.6 1.4 convolution_bitcast_fusion
  65.0 0.0 copy-done
  65.0 1.2 fusion.6
  66.3 0.8 copy.32
  67.1 35.3 %all_to_all.37 = f32[5,4,64,256]{3,1,0,2:T(4,128)S(1)} all-to-all(f32[5,4,64,256]{3,1,0,2:T(4,128)S(1)} %copy.32), channel_id=1, replica_groups=mesh['slab'=16,'grp'=2] {'slab'}, dimensions={2} | all-to-all | bytes 2621440 | tf_op jit(solution)/shard_map/all_to_all | solution.py:54
  102.4 0.3 copy.47
  102.8 1.5 all_to_all.33
  104.3 0.0 copy-start.2
  104.3 0.0 copy-start.4
  104.3 0.0 all-gather.2.cloned.1.call-update
  104.3 0.9 copy-done.2
  105.3 0.1 copy.34
  105.3 37.3 %all-gather.2.cloned.1.call-done = f32[5,128,4,256]{3,1,2,0:T(8,128)} async-done(((f32[5,64,4,256]{3,1,2,0:T(8,128)}), f32[5,128,4,256]{3,1,2,0:T(8,128)}) %all-gather.2.cloned.1.call-update) | async-done | bytes 2621456 | tf_op jit(solution)/shard_map/all_gather | solution.py:58
  142.6 0.0 copy-done.4
  142.6 3.3 %fusion = f32[5,64,4,256]{3,1,2,0:T(8,128)S(1)} fusion(f32[5,128,4,256]{3,1,2,0:T(8,128)} %all-gather.2.cloned.1.call-done, f32[64,4,256]{2,0,1:T(8,128)S(1)} %copy.34, f32[128,64]{0,1:T(8,128)S(1)} %copy-done.4), kind=kOutput, calls=%fused_computation.5 | convolution fusion | flops 503644160 | bytes 4227072 | tf_op jit(solution)/shard_map/jk,cjzy->ckzy/dot_general | solution.py:55
  146.0 0.0 copy-start.1
  146.0 3.8 %collective-permute-start = (f32[5,64,1,256]{3,1,2,0:T(8,128)S(1)}, f32[5,64,1,256]{3,1,2,0:T(8,128)S(1)}, u32[]{:S(2)}, u32[]{:S(2)}) collective-permute-start(f32[5,64,1,256]{3,1,2,0:T(8,128)S(1)} %get-tuple-element.19), channel_id=1, source_target_pairs={{0,2},{2,4},{4,6},{6,8},{8,10},{10,12},{12,14},{14,16},{16,18},{18... | collective-permute-start | bytes 983048 | tf_op jit(solution)/shard_map/ppermute | solution.py:18
  149.8 1.9 %collective-permute-start.1 = (f32[5,64,1,256]{3,1,2,0:T(8,128)S(1)}, f32[5,64,1,256]{3,1,2,0:T(8,128)S(1)}, u32[]{:S(2)}, u32[]{:S(2)}) collective-permute-start(f32[5,64,1,256]{3,1,2,0:T(8,128)S(1)} %get-tuple-element.20), channel_id=1, source_target_pairs={{2,0},{4,2},{6,4},{8,6},{10,8},{12,10},{14,12},{16,14},{18,16},{20... | collective-permute-start | bytes 983048 | tf_op jit(solution)/shard_map/ppermute | solution.py:20
  151.7 0.0 copy-done.1
  151.7 0.1 convert_element_type.12
  151.9 1.9 %collective-permute-done = f32[5,64,1,256]{3,1,2,0:T(8,128)S(1)} collective-permute-done((f32[5,64,1,256]{3,1,2,0:T(8,128)S(1)}, f32[5,64,1,256]{3,1,2,0:T(8,128)S(1)}, u32[]{:S(2)}, u32[]{:S(2)}) %collective-permute-start) | collective-permute-done | bytes 327712 | tf_op jit(solution)/shard_map/ppermute | solution.py:18
  153.8 4.7 %collective-permute-done.1 = f32[5,64,1,256]{3,1,2,0:T(8,128)S(1)} collective-permute-done((f32[5,64,1,256]{3,1,2,0:T(8,128)S(1)}, f32[5,64,1,256]{3,1,2,0:T(8,128)S(1)}, u32[]{:S(2)}, u32[]{:S(2)}) %collective-permute-start.1) | collective-permute-done | bytes 327712 | tf_op jit(solution)/shard_map/ppermute | solution.py:20
  158.5 1.3 collective-permute-start.2
  159.8 0.0 copy-start.3
  159.9 4.1 %collective-permute-start.3 = (f32[5,1,6,256]{3,1,2,0:T(1,128)S(1)}, f32[5,1,6,256]{3,1,2,0:T(1,128)S(1)}, u32[]{:S(2)}, u32[]{:S(2)}) collective-permute-start(f32[5,1,6,256]{3,1,2,0:T(1,128)S(1)} %get-tuple-element.17), channel_id=1, source_target_pairs={{0,1},{2,3},{4,5},{6,7},{8,9},{10,11},{12,13},{14,15},{16,17},{18,... | collective-permute-start | bytes 92168 | tf_op jit(solution)/shard_map/ppermute | solution.py:18
  164.0 0.2 fusion.4
  164.2 0.1 copy.35
  164.2 0.1 copy.36
  164.3 0.1 copy.37
  164.4 0.0 copy-done.3
  164.4 0.0 collective-permute-done.2
  164.4 0.6 collective-permute-done.3
  165.0 2.0 %multiply_add_fusion = f32[5,64,4,256]{3,1,2,0:T(8,128)S(1)} fusion(f32[5,64,4,256]{3,1,2,0:T(8,128)S(1)} %fusion, f32[5,64,1,256]{3,1,2,0:T(8,128)S(1)} %collective-permute-done.1, f32[5,64,1,256]{3,1,2,0:T(8,128)S(1)} %collective-permute-done, f32[5,1,6,256]{3,1,2,0:T(1,128)S(1)} %collective-permute-done.2, ...), kind=kLoop, calls=%fused_computation.16 | loop fusion | flops 8847360 | bytes 4386816 | tf_op jit(solution)/shard_map/add | solution.py:80
  166.9 1.9 %copy.39 = f32[5,64,4,256]{3,2,1,0:T(4,128)} copy(f32[5,64,4,256]{3,1,2,0:T(8,128)S(1)} %multiply_add_fusion) | data formatting | bytes 2621440 | tf_op jit(solution)/shard_map/add | solution.py:80
  (4 shorter events, 0.2 us)
Async XLA Ops:
  6.5 58.5 %copy-start = (f32[256,256]{1,0:T(8,128)S(1)}, f32[256,256]{1,0:T(8,128)}, u32[]{:S(2)}) copy-start(f32[256,256]{1,0:T(8,128)} %param.22) | copy-start | bytes 786436
  6.5 136.1 %all-gather.2.cloned.1.call-start = ((), (), s32[]{:S(2)}) async-start(), calls=%async_computation.2 | async-start | bytes 3932160 | tf_op jit(solution)/shard_map/all_gather | solution.py:58
  62.8 0.8 copy-start.5
  104.3 0.9 copy-start.2
  104.3 38.4 %copy-start.4 = (f32[128,64]{0,1:T(8,128)S(1)}, f32[128,64]{0,1:T(8,128)}, u32[]{:S(2)}) copy-start(f32[128,64]{0,1:T(8,128)} %param.21) | copy-start | bytes 98308
  146.0 5.8 %copy-start.1 = (bf16[3,64,4,256]{3,2,1,0:T(4,128)(2,1)S(1)}, bf16[3,64,4,256]{3,2,1,0:T(4,128)(2,1)}, u32[]{:S(2)}) copy-start(bf16[3,64,4,256]{3,2,1,0:T(4,128)(2,1)} %param.14) | copy-start | bytes 1179652
  146.0 7.8 %collective-permute-start = (f32[5,64,1,256]{3,1,2,0:T(8,128)S(1)}, f32[5,64,1,256]{3,1,2,0:T(8,128)S(1)}, u32[]{:S(2)}, u32[]{:S(2)}) collective-permute-start(f32[5,64,1,256]{3,1,2,0:T(8,128)S(1)} %get-tuple-element.19), channel_id=1, source_target_pairs={{0,2},{2,4},{4,6},{6,8},{8,10},{10,12},{12,14},{14,16},{16,18},{18... | collective-permute-start | bytes 983048 | tf_op jit(solution)/shard_map/ppermute | solution.py:18
  149.8 8.7 %collective-permute-start.1 = (f32[5,64,1,256]{3,1,2,0:T(8,128)S(1)}, f32[5,64,1,256]{3,1,2,0:T(8,128)S(1)}, u32[]{:S(2)}, u32[]{:S(2)}) collective-permute-start(f32[5,64,1,256]{3,1,2,0:T(8,128)S(1)} %get-tuple-element.20), channel_id=1, source_target_pairs={{2,0},{4,2},{6,4},{8,6},{10,8},{12,10},{14,12},{16,14},{18,16},{20... | collective-permute-start | bytes 983048 | tf_op jit(solution)/shard_map/ppermute | solution.py:20
  158.5 5.9 %collective-permute-start.2 = (f32[5,1,6,256]{3,1,2,0:T(1,128)S(1)}, f32[5,1,6,256]{3,1,2,0:T(1,128)S(1)}, u32[]{:S(2)}, u32[]{:S(2)}) collective-permute-start(f32[5,1,6,256]{3,1,2,0:T(1,128)S(1)} %get-tuple-element.18), channel_id=1, source_target_pairs={{1,0},{3,2},{5,4},{7,6},{9,8},{11,10},{13,12},{15,14},{17,16},{19,... | collective-permute-start | bytes 92168 | tf_op jit(solution)/shard_map/ppermute | solution.py:20
  159.8 4.5 %copy-start.3 = (bf16[64,4,256]{2,1,0:T(4,128)(2,1)S(1)}, bf16[64,4,256]{2,1,0:T(4,128)(2,1)}, u32[]{:S(2)}) copy-start(bf16[64,4,256]{2,1,0:T(4,128)(2,1)} %param.15) | copy-start | bytes 393220
  159.9 5.1 %collective-permute-start.3 = (f32[5,1,6,256]{3,1,2,0:T(1,128)S(1)}, f32[5,1,6,256]{3,1,2,0:T(1,128)S(1)}, u32[]{:S(2)}, u32[]{:S(2)}) collective-permute-start(f32[5,1,6,256]{3,1,2,0:T(1,128)S(1)} %get-tuple-element.17), channel_id=1, source_target_pairs={{0,1},{2,3},{4,5},{6,7},{8,9},{10,11},{12,13},{14,15},{16,17},{18,... | collective-permute-start | bytes 92168 | tf_op jit(solution)/shard_map/ppermute | solution.py:18
Sparse Core Ops, SparseCore 0:
  104.4 38.1 all-gather.1
where the time goes:
time: 176 us
  blocking collectives  74.3 us (42%)
  waiting for transfers between devices  44.5 us (25%)
  other arithmetic  17.9 us (10%)
  between operations  13.6 us (8%)
  starting transfers between devices  11.1 us (6%)
  local copies, waits for them, and re-layouts  8.25 us (5%)
  matrix products  5.94 us (3%)
    all_to_all x1, blocking collectives, body(): lax.all_to_all(seeded, 'slab', split_axis=1, concat_axis=2, tiled=True)  39 us
    all_gather x1, waiting for transfers between devices, body(): lax.all_gather(returned, 'grp', axis=1, tiled=True)  37.3 us
    all_to_all x1, blocking collectives, body(): lax.all_to_all(zlines, 'slab', split_axis=2, concat_axis=1, tiled=True)  35.3 us
    scatter-add x1, other arithmetic, body(): jax.ops.segment_sum(jnp.where(inside, drag_weight, 0.0), flat_index, num_...  14 us
    ppermute x2, starting transfers between devices, extended(): lax.ppermute(tail, axis, [(i, (i + 1) % count) for i in range(ends)])  7.9 us
    ppermute x2, waiting for transfers between devices, extended(): lax.ppermute(head, axis, [((i + 1) % count, i) for i in range(ends)])  4.69 us
  transfers between devices with their start and end apart: 5, of which 4 were waited for; matrix products, arithmetic and copies ran while one was open for 0% of the time, Pallas kernels for 0%

commit v1 on v0

v1 whole, which is shorter than its diff:
```python
import jax
import jax.numpy as jnp
from jax import lax
from jax.sharding import PartitionSpec as P

time_step = 0.08
highest = lax.Precision.HIGHEST


def neighbours(cells, axis, dim):
    count = lax.axis_size(axis)
    ends = count - 1
    head = lax.slice_in_dim(cells, 0, 1, axis=dim)
    tail = lax.slice_in_dim(cells, cells.shape[dim] - 1, cells.shape[dim], axis=dim)
    before = lax.ppermute(tail, axis, [(i, i + 1) for i in range(ends)])
    after = lax.ppermute(head, axis, [(i + 1, i) for i in range(ends)])
    return before, after


def shifted(cells, before, after, dim):
    size = cells.shape[dim]
    down = jnp.concatenate([before, lax.slice_in_dim(cells, 0, size - 1, axis=dim)], axis=dim)
    up = jnp.concatenate([lax.slice_in_dim(cells, 1, size, axis=dim), after], axis=dim)
    return down, up


def marker_push(shape, marker_x, marker_z, marker_y, drag_weight):
    x_rows, z_rows, y_cells = shape
    local_x = marker_x - lax.axis_index("grp") * x_rows
    local_z = marker_z - lax.axis_index("slab") * z_rows
    inside = (local_x >= 0) & (local_x < x_rows) & (local_z >= 0) & (local_z < z_rows)
    row = jnp.where(inside, local_x * z_rows + local_z, -1)
    at_row = (jnp.arange(x_rows * z_rows)[:, None] == row[None, :]).astype(jnp.float32)
    at_y = jnp.where(marker_y[:, None] == jnp.arange(y_cells)[None, :], drag_weight[:, None], 0.0)
    return jnp.dot(at_row, at_y, precision=highest).reshape(shape)


def to_lines(cells):
    return lax.all_to_all(cells, "slab", split_axis=1, concat_axis=2, tiled=True)


def to_cells(lines):
    return lax.all_to_all(lines, "slab", split_axis=2, concat_axis=1, tiled=True)


def solve_zy(lines, inv_z, inv_y):
    lines = jnp.einsum("jk,cxjy->cxky", inv_z, lines, precision=highest)
    return jnp.einsum("jk,cxzj->cxzk", inv_y, lines, precision=highest)


def solve_x(cells, inv_x):
    return jnp.einsum(
        "jk,cjzy->ckzy", inv_x, lax.all_gather(cells, "grp", axis=1, tiled=True), precision=highest
    )


def body(
    adj_out,
    advect,
    viscosity,
    body_mask,
    marker_x,
    marker_z,
    marker_y,
    drag_weight,
    inv_x,
    inv_y,
    inv_z,
):
    fields, x_rows, z_rows, y_cells = adj_out.shape
    split = fields - fields // 2
    last = adj_out[split:]
    last = solve_x(last, inv_x)
    pushed = marker_push((x_rows, z_rows, y_cells), marker_x, marker_z, marker_y, drag_weight)
    first = adj_out[:split].at[0].add(pushed)
    first = solve_zy(to_lines(first), inv_z, inv_y)
    last = to_lines(last)
    first, last = lax.optimization_barrier((to_cells(first), last))
    last = to_cells(solve_zy(last, inv_z, inv_y))
    first = solve_x(first, inv_x)
    fluid = body_mask.astype(jnp.float32)
    masked = jnp.concatenate([first, last], axis=0) * fluid
    z_before, z_after = neighbours(masked, "slab", 2)
    x_before, x_after = neighbours(masked, "grp", 1)
    x_down, x_up = shifted(masked, x_before, x_after, 1)
    z_down, z_up = shifted(masked, z_before, z_after, 2)
    y_edge = jnp.zeros_like(masked[..., :1])
    y_down, y_up = shifted(masked, y_edge, y_edge, 3)
    grad_x = (x_up - x_down) * 0.5
    grad_z = (z_up - z_down) * 0.5
    grad_y = (y_up - y_down) * 0.5
    laplace = x_up + x_down + z_up + z_down + y_up + y_down - 6.0 * masked
    velocity = advect.astype(jnp.float32)
    viscous = viscosity.astype(jnp.float32)
    change = velocity[0] * grad_x + velocity[1] * grad_z + velocity[2] * grad_y + viscous * laplace
    return masked + time_step * change


def solution(mesh):
    in_specs = (
        P(None, "grp", "slab", None),
        P(None, "grp", "slab", None),
        P("grp", "slab", None),
        P("grp", "slab", None),
        P(),
        P(),
        P(),
        P(),
        P(None, "grp"),
        P(),
        P(),
    )
    out_specs = P(None, "grp", "slab", None)
    return jax.shard_map(body, mesh=mesh, in_specs=in_specs, out_specs=out_specs, check_vma=False)
```

time: 176 us -> 146 us (0.83)
  blocking collectives: 74.3 us -> 0 us
  waiting for transfers between devices: 44.5 us -> 71.1 us
  starting transfers between devices: 11.1 us -> 35.2 us
  other arithmetic: 17.9 us -> 3.21 us
  local copies, waits for them, and re-layouts: 8.25 us -> 12.3 us
  matrix products: 5.94 us -> 9.62 us
    all_to_all x2 -> x0, blocking collectives: 74.3 us -> none  [the longest x1 39 us: body(): lax.all_to_all(seeded, 'slab', split_axis=1, concat_axis=2, tiled=True)]
    all_to_all x0 -> x4, waiting for transfers between devices: none -> 42.4 us  [the longest x2 31.7 us: to_cells(): lax.all_to_all(lines, 'slab', split_axis=2, concat_axis=1, tiled=True)]
    all_to_all x0 -> x4, starting transfers between devices: none -> 24 us  [the longest x2 13.8 us: to_lines(): lax.all_to_all(cells, 'slab', split_axis=1, concat_axis=2, tiled=True)]
    scatter-add x2 -> x1, other arithmetic: 14 us -> 0.77 us  [body(): first = adj_out[:split].at[0].add(pushed)]
    all_gather x1 -> x2, waiting for transfers between devices: 37.3 us -> 27.9 us  [solve_x(): lax.all_gather(cells, 'grp', axis=1, tiled=True)]
    ppermute x4, waiting for transfers between devices: 7.2 us -> 0.74 us  [the longest x2 0.74 us: neighbours(): before = lax.ppermute(tail, axis, [(i, i + 1) for i in range(ends)])]
    dot_general x3 -> x7, matrix products: 5.94 us -> 9.62 us  [the longest x2 4.33 us: solve_x(): jnp.einsum('jk,cjzy->ckzy', inv_x, lax.all_gather(cells, 'grp', axis=1, t...]
    slice x1 -> x9, local copies, waits for them, and re-layouts: 0.05 us -> 2.47 us  [the longest x2 1.43 us: body(): first = adj_out[:split].at[0].add(pushed)]
  transfers between devices with their start and end apart: 5 -> 10, of which waited for: 4 -> 7; matrix products, arithmetic and copies ran while one was open for 0% -> 7% of each run, Pallas kernels for 0% -> 0%
where the time goes in v1:
time: 146 us; the launch traced here: 145 us
  waiting for transfers between devices  71.1 us (49%)
  starting transfers between devices  35.2 us (24%)
  between operations  13.7 us (9%)
  local copies, waits for them, and re-layouts  12.3 us (8%)
  matrix products  9.62 us (7%)
  other arithmetic  3.21 us (2%)
    all_to_all x2, waiting for transfers between devices, to_cells(): lax.all_to_all(lines, 'slab', split_axis=2, concat_axis=1, tiled=True)  31.7 us
    all_gather x2, waiting for transfers between devices, solve_x(): lax.all_gather(cells, 'grp', axis=1, tiled=True)  27.9 us
    all_to_all x2, starting transfers between devices, to_lines(): lax.all_to_all(cells, 'slab', split_axis=1, concat_axis=2, tiled=True)  13.8 us
    all_to_all x2, waiting for transfers between devices, to_lines(): lax.all_to_all(cells, 'slab', split_axis=1, concat_axis=2, tiled=True)  10.7 us
    all_to_all x2, starting transfers between devices, to_cells(): lax.all_to_all(lines, 'slab', split_axis=2, concat_axis=1, tiled=True)  10.3 us
    ppermute x2, starting transfers between devices, neighbours(): before = lax.ppermute(tail, axis, [(i, i + 1) for i in range(ends)])  7.16 us
    dot_general x2, matrix products, solve_x(): jnp.einsum('jk,cjzy->ckzy', inv_x, lax.all_gather(cells, 'grp', axis=1, t...  4.33 us
    ppermute x2, starting transfers between devices, neighbours(): after = lax.ppermute(head, axis, [(i + 1, i) for i in range(ends)])  3.88 us
  transfers between devices with their start and end apart: 10, of which 7 were waited for; matrix products, arithmetic and copies ran while one was open for 7% of the time, Pallas kernels for 0%

profile of v1, /device:TPU:1, one launch (start us, length us, event | category | flops | bytes accessed | tf_op | source)
XLA Modules:
  0.0 145.1 jit_solution(12885374733892964591)
XLA Ops:
  6.5 0.8 add_select_fusion
  7.3 2.4 %fusion = f32[256,256]{1,0:T(8,128)S(1)} fusion(f32[2048]{0:T(1024)} %param.20, s32[2048]{0:T(1024)} %param.19, s32[2048]{0:T(1024)S(1)} %add_select_fusion), kind=kOutput, calls=%fused_computation | convolution fusion | flops 1612185600 | bytes 286720 | tf_op jit(solution)/shard_map/dot_general | solution.py:35
  9.7 0.1 reshape.50
  9.8 1.4 slice-done
  11.2 1.0 copy.59
  12.2 0.8 fusion.11
  13.0 7.5 %all-to-all-start = ((f32[3,64,4,256]{3,2,0,1:T(4,128)}), f32[3,64,4,256]{3,2,0,1:T(4,128)S(1)}, u32[]{:S(2)}, u32[]{:S(2)}) async-start(f32[3,64,4,256]{3,2,0,1:T(4,128)} %fusion.11), calls=%async_computation | async-start | bytes 1572864 | tf_op jit(solution)/shard_map/all_to_all | solution.py:39
  20.5 0.9 copy.61
  21.4 23.5 %all-gather.3.cloned.1.call-done = f32[2,128,4,256]{3,1,2,0:T(8,128)} async-done(((f32[2,64,4,256]{3,1,2,0:T(8,128)}), f32[2,128,4,256]{3,1,2,0:T(8,128)}) %all-gather.3.cloned.1.call-update) | async-done | bytes 1048592 | tf_op jit(solution)/shard_map/all_gather | solution.py:53
  45.0 1.9 %convolution_bitcast_fusion.3 = f32[2,64,4,256]{3,1,2,0:T(8,128)S(1)} fusion(f32[2,128,4,256]{3,1,2,0:T(8,128)} %all-gather.3.cloned.1.call-done, f32[128,64]{0,1:T(8,128)S(1)} %copy-done.4), kind=kOutput, calls=%fused_computation.13 | convolution fusion | flops 201326592 | bytes 1605632 | tf_op jit(solution)/shard_map/jk,cjzy->ckzy/dot_general | solution.py:52
  46.9 1.1 copy.41
  48.0 6.3 %all-to-all-start.2 = ((f32[2,64,4,256]{3,2,0,1:T(4,128)}), f32[2,64,4,256]{3,2,0,1:T(4,128)S(1)}, u32[]{:S(2)}, u32[]{:S(2)}) async-start(f32[2,64,4,256]{3,2,0,1:T(4,128)} %copy.41), calls=%async_computation.2 | async-start | bytes 1048576 | tf_op jit(solution)/shard_map/all_to_all | solution.py:39
  54.4 0.2 copy.35
  54.6 0.9 convolution_bitcast_fusion.1
  55.6 0.8 fusion.14
  56.3 1.4 copy.38
  57.7 10.7 %all-to-all-done.2 = f32[2,64,4,256]{3,2,0,1:T(4,128)S(1)} async-done(((f32[2,64,4,256]{3,2,0,1:T(4,128)}), f32[2,64,4,256]{3,2,0,1:T(4,128)S(1)}, u32[]{:S(2)}, u32[]{:S(2)}) %all-to-all-start.2) | async-done | bytes 524320 | tf_op jit(solution)/shard_map/all_to_all | solution.py:39
  68.4 4.5 %all-to-all-start.1 = ((f32[3,4,64,256]{3,1,0,2:T(4,128)}), f32[3,4,64,256]{3,1,0,2:T(4,128)S(1)}, u32[]{:S(2)}, u32[]{:S(2)}) async-start(f32[3,4,64,256]{3,1,0,2:T(4,128)} %copy.38), calls=%async_computation.1 | async-start | bytes 1572864 | tf_op jit(solution)/shard_map/all_to_all | solution.py:43
  73.0 0.2 copy.42
  73.2 18.3 %all-to-all-done.1 = f32[3,4,64,256]{3,1,0,2:T(4,128)S(1)} async-done(((f32[3,4,64,256]{3,1,0,2:T(4,128)}), f32[3,4,64,256]{3,1,0,2:T(4,128)S(1)}, u32[]{:S(2)}, u32[]{:S(2)}) %all-to-all-start.1) | async-done | bytes 786464 | tf_op jit(solution)/shard_map/all_to_all | solution.py:43
  91.5 0.2 copy.68
  91.7 1.2 all_to_all.59
  92.9 0.7 convolution_bitcast_fusion.2
  93.5 0.6 fusion.12
  94.1 1.1 copy.45
  95.3 5.8 %all-to-all-start.3 = ((f32[2,4,64,256]{3,1,0,2:T(4,128)}), f32[2,4,64,256]{3,1,0,2:T(4,128)S(1)}, u32[]{:S(2)}, u32[]{:S(2)}) async-start(f32[2,4,64,256]{3,1,0,2:T(4,128)} %copy.45), calls=%async_computation.3 | async-start | bytes 1048576 | tf_op jit(solution)/shard_map/all_to_all | solution.py:43
  101.1 0.1 copy.47
  101.2 0.1 convert_element_type.11
  101.3 0.2 fusion.10
  101.5 0.1 copy.48
  101.6 0.1 copy.50
  101.6 0.1 copy.49
  101.7 13.4 %all-to-all-done.3 = f32[2,4,64,256]{3,1,0,2:T(4,128)S(1)} async-done(((f32[2,4,64,256]{3,1,0,2:T(4,128)}), f32[2,4,64,256]{3,1,0,2:T(4,128)S(1)}, u32[]{:S(2)}, u32[]{:S(2)}) %all-to-all-start.3) | async-done | bytes 524320 | tf_op jit(solution)/shard_map/all_to_all | solution.py:43
  115.1 0.2 all_to_all.67
  115.3 4.3 %all-gather.5.cloned.1.call-done = f32[3,128,4,256]{3,1,2,0:T(8,128)} async-done(((f32[3,64,4,256]{3,1,2,0:T(8,128)}), f32[3,128,4,256]{3,1,2,0:T(8,128)}) %all-gather.5.cloned.1.call-update) | async-done | bytes 1572880 | tf_op jit(solution)/shard_map/all_gather | solution.py:53
  119.7 2.4 %convolution_bitcast_fusion = f32[3,64,4,256]{3,1,2,0:T(8,128)S(1)} fusion(f32[3,128,4,256]{3,1,2,0:T(8,128)} %all-gather.5.cloned.1.call-done, f32[128,64]{0,1:T(8,128)S(1)} %copy-done.4), kind=kOutput, calls=%fused_computation.10 | convolution fusion | flops 301989888 | bytes 2392064 | tf_op jit(solution)/shard_map/jk,cjzy->ckzy/dot_general | solution.py:52
  122.1 0.1 maximum_multiply_fusion
  122.2 0.4 fusion.25
  122.7 0.3 fusion.21
  123.0 2.6 %collective-permute-start.2 = (f32[5,64,1,256]{3,1,2,0:T(8,128)S(1)}, f32[5,64,1,256]{3,1,2,0:T(8,128)S(1)}, u32[]{:S(2)}, u32[]{:S(2)}) collective-permute-start(f32[5,64,1,256]{3,1,2,0:T(8,128)S(1)} %get-tuple-element.27), channel_id=1, source_target_pairs={{2,0},{4,2},{6,4},{8,6},{10,8},{12,10},{14,12},{16,14},{18,16},{20... | collective-permute-start | bytes 983048 | tf_op jit(solution)/shard_map/ppermute | solution.py:16
  125.6 3.2 %collective-permute-start.3 = (f32[5,64,1,256]{3,1,2,0:T(8,128)S(1)}, f32[5,64,1,256]{3,1,2,0:T(8,128)S(1)}, u32[]{:S(2)}, u32[]{:S(2)}) collective-permute-start(f32[5,64,1,256]{3,1,2,0:T(8,128)S(1)} %get-tuple-element.28), channel_id=1, source_target_pairs={{0,2},{2,4},{4,6},{6,8},{8,10},{10,12},{12,14},{14,16},{16,18},{18... | collective-permute-start | bytes 983048 | tf_op jit(solution)/shard_map/ppermute | solution.py:15
  128.8 1.3 collective-permute-start
  130.1 4.0 %collective-permute-start.1 = (f32[5,1,4,256]{3,1,2,0:T(1,128)S(1)}, f32[5,1,4,256]{3,1,2,0:T(1,128)S(1)}, u32[]{:S(2)}, u32[]{:S(2)}) collective-permute-start(f32[5,1,4,256]{3,1,2,0:T(1,128)S(1)} %get-tuple-element.24), channel_id=1, source_target_pairs={{0,1},{2,3},{4,5},{6,7},{8,9},{10,11},{12,13},{14,15},{16,17},{18,... | collective-permute-start | bytes 61448 | tf_op jit(solution)/shard_map/ppermute | solution.py:15
  134.1 0.2 fusion.23
  134.4 0.7 collective-permute-done.1
  135.0 0.1 collective-permute-done.3
  135.1 1.2 multiply_add_fusion
  136.3 1.9 %copy.52 = f32[5,64,4,256]{3,2,1,0:T(4,128)} copy(f32[5,64,4,256]{3,1,2,0:T(8,128)S(1)} %multiply_add_fusion) | data formatting | bytes 2621440 | tf_op jit(solution)/shard_map/add | solution.py:96
  (29 shorter events, 0.3 us)
Async XLA Ops:
  6.5 49.0 %copy-start = (f32[256,256]{1,0:T(8,128)S(1)}, f32[256,256]{1,0:T(8,128)}, u32[]{:S(2)}) copy-start(f32[256,256]{1,0:T(8,128)} %param.22) | copy-start | bytes 786436
  9.7 1.5 %slice-start = ((f32[5,64,4,256]{3,2,1,0:T(4,128)}), f32[3,64,4,256]{3,2,1,0:T(4,128)S(1)}, s32[]{:S(2)}) async-start(f32[5,64,4,256]{3,2,1,0:T(4,128)} %param.13), calls=%async_computation.6 | async-start | bytes 1572864 | tf_op jit(solution)/shard_map/slice | solution.py:75
  9.8 2.5 %copy-start.1 = (f32[5,64,4,256]{3,2,1,0:T(4,128)S(1)}, f32[5,64,4,256]{3,2,1,0:T(4,128)}, u32[]{:S(2)}) copy-start(f32[5,64,4,256]{3,2,1,0:T(4,128)} %param.13) | copy-start | bytes 3932164
  13.0 7.5 %slice-start.1 = ((f32[5,64,4,256]{3,2,1,0:T(4,128)}), f32[2,64,4,256]{3,2,1,0:T(4,128)S(1)}, s32[]{:S(2)}) async-start(f32[5,64,4,256]{3,2,1,0:T(4,128)} %param.13), calls=%async_computation.7 | async-start | bytes 1048576 | tf_op jit(solution)/shard_map/slice | solution.py:72
  13.0 35.0 %all-to-all-start = ((f32[3,64,4,256]{3,2,0,1:T(4,128)}), f32[3,64,4,256]{3,2,0,1:T(4,128)S(1)}, u32[]{:S(2)}, u32[]{:S(2)}) async-start(f32[3,64,4,256]{3,2,0,1:T(4,128)} %fusion.11), calls=%async_computation | async-start | bytes 1572864 | tf_op jit(solution)/shard_map/all_to_all | solution.py:39
  20.4 24.5 %copy-start.4 = (f32[128,64]{0,1:T(8,128)S(1)}, f32[128,64]{0,1:T(8,128)}, u32[]{:S(2)}) copy-start(f32[128,64]{0,1:T(8,128)} %param.21) | copy-start | bytes 98308
  20.5 24.5 %all-gather.3.cloned.1.call-start = ((), (), s32[]{:S(2)}) async-start(), calls=%async_computation.4 | async-start | bytes 1572864 | tf_op jit(solution)/shard_map/all_gather | solution.py:53
  48.0 6.6 %copy-start.6 = (f32[64,64]{1,0:T(8,128)S(1)}, f32[64,64]{1,0:T(8,128)}, u32[]{:S(2)}) copy-start(f32[64,64]{1,0:T(8,128)} %param.23) | copy-start | bytes 49156
  48.0 20.4 %all-to-all-start.2 = ((f32[2,64,4,256]{3,2,0,1:T(4,128)}), f32[2,64,4,256]{3,2,0,1:T(4,128)S(1)}, u32[]{:S(2)}, u32[]{:S(2)}) async-start(f32[2,64,4,256]{3,2,0,1:T(4,128)} %copy.41), calls=%async_computation.2 | async-start | bytes 1048576 | tf_op jit(solution)/shard_map/all_to_all | solution.py:39
  68.4 23.1 %all-to-all-start.1 = ((f32[3,4,64,256]{3,1,0,2:T(4,128)}), f32[3,4,64,256]{3,1,0,2:T(4,128)S(1)}, u32[]{:S(2)}, u32[]{:S(2)}) async-start(f32[3,4,64,256]{3,1,0,2:T(4,128)} %copy.38), calls=%async_computation.1 | async-start | bytes 1572864 | tf_op jit(solution)/shard_map/all_to_all | solution.py:43
  72.9 46.7 %all-gather.5.cloned.1.call-start = ((), (), s32[]{:S(2)}) async-start(), calls=%async_computation.5 | async-start | bytes 2359296 | tf_op jit(solution)/shard_map/all_gather | solution.py:53
  94.1 6.9 %copy-start.5 = (bf16[64,4,256]{2,1,0:T(4,128)(2,1)S(1)}, bf16[64,4,256]{2,1,0:T(4,128)(2,1)}, u32[]{:S(2)}) copy-start(bf16[64,4,256]{2,1,0:T(4,128)(2,1)} %param.15) | copy-start | bytes 393220
  94.1 6.9 %copy-start.3 = (s32[64,4,256]{2,1,0:T(4,128)S(1)}, s32[64,4,256]{2,1,0:T(4,128)}, u32[]{:S(2)}) copy-start(s32[64,4,256]{2,1,0:T(4,128)} %param.16) | copy-start | bytes 786436
  95.3 5.9 %copy-start.2 = (bf16[3,64,4,256]{3,2,1,0:T(4,128)(2,1)S(1)}, bf16[3,64,4,256]{3,2,1,0:T(4,128)(2,1)}, u32[]{:S(2)}) copy-start(bf16[3,64,4,256]{3,2,1,0:T(4,128)(2,1)} %param.14) | copy-start | bytes 1179652
  95.3 19.8 %all-to-all-start.3 = ((f32[2,4,64,256]{3,1,0,2:T(4,128)}), f32[2,4,64,256]{3,1,0,2:T(4,128)S(1)}, u32[]{:S(2)}, u32[]{:S(2)}) async-start(f32[2,4,64,256]{3,1,0,2:T(4,128)} %copy.45), calls=%async_computation.3 | async-start | bytes 1048576 | tf_op jit(solution)/shard_map/all_to_all | solution.py:43
  123.0 12.0 %collective-permute-start.2 = (f32[5,64,1,256]{3,1,2,0:T(8,128)S(1)}, f32[5,64,1,256]{3,1,2,0:T(8,128)S(1)}, u32[]{:S(2)}, u32[]{:S(2)}) collective-permute-start(f32[5,64,1,256]{3,1,2,0:T(8,128)S(1)} %get-tuple-element.27), channel_id=1, source_target_pairs={{2,0},{4,2},{6,4},{8,6},{10,8},{12,10},{14,12},{16,14},{18,16},{20... | collective-permute-start | bytes 983048 | tf_op jit(solution)/shard_map/ppermute | solution.py:16
  125.6 9.5 %collective-permute-start.3 = (f32[5,64,1,256]{3,1,2,0:T(8,128)S(1)}, f32[5,64,1,256]{3,1,2,0:T(8,128)S(1)}, u32[]{:S(2)}, u32[]{:S(2)}) collective-permute-start(f32[5,64,1,256]{3,1,2,0:T(8,128)S(1)} %get-tuple-element.28), channel_id=1, source_target_pairs={{0,2},{2,4},{4,6},{6,8},{8,10},{10,12},{12,14},{14,16},{16,18},{18... | collective-permute-start | bytes 983048 | tf_op jit(solution)/shard_map/ppermute | solution.py:15
  128.8 5.5 %collective-permute-start = (f32[5,1,4,256]{3,1,2,0:T(1,128)S(1)}, f32[5,1,4,256]{3,1,2,0:T(1,128)S(1)}, u32[]{:S(2)}, u32[]{:S(2)}) collective-permute-start(f32[5,1,4,256]{3,1,2,0:T(1,128)S(1)} %get-tuple-element.23), channel_id=1, source_target_pairs={{1,0},{3,2},{5,4},{7,6},{9,8},{11,10},{13,12},{15,14},{17,16},{19,... | collective-permute-start | bytes 61448 | tf_op jit(solution)/shard_map/ppermute | solution.py:16
  130.1 4.9 %collective-permute-start.1 = (f32[5,1,4,256]{3,1,2,0:T(1,128)S(1)}, f32[5,1,4,256]{3,1,2,0:T(1,128)S(1)}, u32[]{:S(2)}, u32[]{:S(2)}) collective-permute-start(f32[5,1,4,256]{3,1,2,0:T(1,128)S(1)} %get-tuple-element.24), channel_id=1, source_target_pairs={{0,1},{2,3},{4,5},{6,7},{8,9},{10,11},{12,13},{14,15},{16,17},{18,... | collective-permute-start | bytes 61448 | tf_op jit(solution)/shard_map/ppermute | solution.py:15
Sparse Core Ops, SparseCore 0:
  22.8 22.0 all-gather.2
  93.0 26.6 all-gather.4

commit v2 on v1

--- a/solution.py
+++ b/solution.py
@@ -1,6 +1,10 @@
+import functools
+
 import jax
 import jax.numpy as jnp
 from jax import lax
+from jax.experimental import pallas as pl
+from jax.experimental.pallas import tpu as pltpu
 from jax.sharding import PartitionSpec as P
 
 time_step = 0.08
@@ -35,23 +39,142 @@
     return jnp.dot(at_row, at_y, precision=highest).reshape(shape)
 
 
-def to_lines(cells):
-    return lax.all_to_all(cells, "slab", split_axis=1, concat_axis=2, tiled=True)
-
-
-def to_cells(lines):
-    return lax.all_to_all(lines, "slab", split_axis=2, concat_axis=1, tiled=True)
-
-
-def solve_zy(lines, inv_z, inv_y):
-    lines = jnp.einsum("jk,cxjy->cxky", inv_z, lines, precision=highest)
-    return jnp.einsum("jk,cxzj->cxzk", inv_y, lines, precision=highest)
-
-
-def solve_x(cells, inv_x):
-    return jnp.einsum(
-        "jk,cjzy->ckzy", inv_x, lax.all_gather(cells, "grp", axis=1, tiled=True), precision=highest
-    )
+def wait_bytes(block, sem):
+    pltpu.make_async_copy(block, block, sem).wait()
+
+
+def send(src, dst, send_sem, recv_sem, axis, to):
+    pltpu.make_async_remote_copy(
+        src_ref=src,
+        dst_ref=dst,
+        send_sem=send_sem,
+        recv_sem=recv_sem,
+        device_id={axis: to},
+        device_id_type=pl.DeviceIdType.MESH,
+    ).start()
+
+
+def solve_kernel(
+    slabs, grps, cells, mat_x, mat_z, mat_y, out,
+    xin, xdone, lines, zdone, ret,
+    x_send, x_recv, l_send, l_recv, r_send, r_recv,
+):
+    fields = cells.shape[0]
+    rows = cells.shape[1] * cells.shape[2]
+    width = cells.shape[3]
+    me = lax.axis_index("slab")
+    mine = lax.axis_index("grp")
+
+    barrier = pltpu.get_barrier_semaphore()
+
+    def greet(axis, here, count):
+        def one(k, carry):
+            pl.semaphore_signal(
+                barrier,
+                inc=1,
+                device_id={axis: lax.rem(here + k, count)},
+                device_id_type=pl.DeviceIdType.MESH,
+            )
+            return carry
+
+        lax.fori_loop(1, count, one, 0)
+
+    greet("slab", me, slabs)
+    greet("grp", mine, grps)
+    pl.semaphore_wait(barrier, slabs + grps - 2)
+
+    for c in range(fields):
+        def to_grp(k, carry):
+            send(cells.at[c], xin.at[c, mine], x_send.at[c], x_recv.at[c], "grp", lax.rem(mine + k, grps))
+            return carry
+
+        lax.fori_loop(1, grps, to_grp, 0)
+
+    def matmul(left, right):
+        return jnp.dot(left, right, precision=highest, preferred_element_type=jnp.float32)
+
+    def x_stage(c):
+        xin[c, mine] = cells[c]
+        wait_bytes(xin.at[c, pl.ds(0, grps - 1)], x_recv.at[c])
+        xdone[c] = matmul(mat_x[...], xin[c].reshape(grps * rows, width)).reshape(cells.shape[1:])
+        lines[c, me] = xdone[c, me]
+
+        def to_slab(k, carry):
+            d = lax.rem(me + k, slabs)
+            send(xdone.at[c, d], lines.at[c, me], l_send.at[c], l_recv.at[c], "slab", d)
+            return carry
+
+        lax.fori_loop(1, slabs, to_slab, 0)
+
+    def z_stage(c):
+        wait_bytes(lines.at[c, pl.ds(0, slabs - 1)], l_recv.at[c])
+        solved = matmul(matmul(mat_z[...], lines[c].reshape(rows, width)), mat_y[...])
+        zdone[c] = solved.reshape(cells.shape[1:])
+        ret[c, me] = zdone[c, me]
+
+        def to_slab(k, carry):
+            d = lax.rem(me + k, slabs)
+            send(zdone.at[c, d], ret.at[c, me], r_send.at[c], r_recv.at[c], "slab", d)
+            return carry
+
+        lax.fori_loop(1, slabs, to_slab, 0)
+
+    for c in range(fields + 2):
+        if c < fields:
+            x_stage(c)
+        if c >= 2:
+            z_stage(c - 2)
+    for c in range(fields):
+        wait_bytes(ret.at[c, pl.ds(0, slabs - 1)], r_recv.at[c])
+        out[c] = ret[c]
+    for c in range(fields):
+        wait_bytes(xin.at[c, pl.ds(0, grps - 1)], x_send.at[c])
+        wait_bytes(lines.at[c, pl.ds(0, slabs - 1)], l_send.at[c])
+        wait_bytes(ret.at[c, pl.ds(0, slabs - 1)], r_send.at[c])
+
+
+def spread(inverse, sources, results):
+    rows, columns = inverse.shape
+    pick_source = (sources[None, :] == jnp.arange(rows)[:, None]).astype(jnp.float32)
+    pick_result = (results[None, :] == jnp.arange(columns)[:, None]).astype(jnp.float32)
+    picked = jnp.einsum("jk,kr->rj", inverse, pick_result, precision=highest)
+    return jnp.dot(picked, pick_source, precision=highest)
+
+
+def solve(seeded, inv_x, inv_y, inv_z):
+    fields, x_rows, z_rows, width = seeded.shape
+    slabs, grps = lax.axis_size("slab"), lax.axis_size("grp")
+    x_part = x_rows // slabs
+    block = (slabs, x_part * z_rows, width)
+    rows = x_rows * z_rows
+    at = jnp.arange(rows)
+    across = jnp.arange(grps * rows)
+    mat_x = spread(inv_x, across // z_rows, at // z_rows)
+    mat_x = jnp.where(at[:, None] % z_rows == across[None, :] % z_rows, mat_x, 0.0)
+    line_z = at // (x_part * z_rows) * z_rows + at % z_rows
+    line_x = at // z_rows % x_part
+    mat_z = spread(inv_z, line_z, line_z)
+    mat_z = jnp.where(line_x[:, None] == line_x[None, :], mat_z, 0.0)
+    whole = pl.BlockSpec(memory_space=pltpu.VMEM)
+    sems = pltpu.SemaphoreType.DMA((fields,))
+    solved = pl.pallas_call(
+        functools.partial(solve_kernel, slabs, grps),
+        out_shape=jax.ShapeDtypeStruct((fields,) + block, jnp.float32),
+        in_specs=[whole] * 4,
+        out_specs=whole,
+        scratch_shapes=[
+            pltpu.VMEM((fields, grps) + block, jnp.float32),
+            pltpu.VMEM((fields,) + block, jnp.float32),
+            pltpu.VMEM((fields,) + block, jnp.float32),
+            pltpu.VMEM((fields,) + block, jnp.float32),
+            pltpu.VMEM((fields,) + block, jnp.float32),
+        ]
+        + [sems] * 6,
+        compiler_params=pltpu.CompilerParams(
+            collective_id=0, has_side_effects=True, vmem_limit_bytes=56 * 1024 * 1024
+        ),
+    )(seeded.reshape((fields,) + block), mat_x, mat_z, inv_y)
+    return solved.reshape(seeded.shape)
 
 
 def body(
@@ -68,18 +191,10 @@
     inv_z,
 ):
     fields, x_rows, z_rows, y_cells = adj_out.shape
-    split = fields - fields // 2
-    last = adj_out[split:]
-    last = solve_x(last, inv_x)
     pushed = marker_push((x_rows, z_rows, y_cells), marker_x, marker_z, marker_y, drag_weight)
-    first = adj_out[:split].at[0].add(pushed)
-    first = solve_zy(to_lines(first), inv_z, inv_y)
-    last = to_lines(last)
-    first, last = lax.optimization_barrier((to_cells(first), last))
-    last = to_cells(solve_zy(last, inv_z, inv_y))
-    first = solve_x(first, inv_x)
+    solved = solve(adj_out.at[0].add(pushed), inv_x, inv_y, inv_z)
     fluid = body_mask.astype(jnp.float32)
-    masked = jnp.concatenate([first, last], axis=0) * fluid
+    masked = solved * fluid
     z_before, z_after = neighbours(masked, "slab", 2)
     x_before, x_after = neighbours(masked, "grp", 1)
     x_down, x_up = shifted(masked, x_before, x_after, 1)

time: 146 us -> 101 us (0.69)
  Pallas kernels: 0 us -> 74.1 us
  waiting for transfers between devices: 71.1 us -> 0.01 us
  starting transfers between devices: 35.2 us -> 10.8 us
  between operations: 13.7 us -> 0.34 us
  matrix products: 9.62 us -> 4.36 us
  local copies, waits for them, and re-layouts: 12.3 us -> 8.4 us
    pallas_call x0 -> x1, Pallas kernels: none -> 74.1 us  [solve(): pl.pallas_call(functools.partial(solve_kernel, slabs, grps), out_shape=ja...]
    all_to_all x4 -> x0, waiting for transfers between devices: 42.4 us -> none  [the longest x2 31.7 us: to_cells(): lax.all_to_all(lines, 'slab', split_axis=2, concat_axis=1, tiled=True)]
    all_gather x2 -> x0, waiting for transfers between devices: 27.9 us -> none  [solve_x(): lax.all_gather(cells, 'grp', axis=1, tiled=True)]
    all_to_all x4 -> x0, starting transfers between devices: 24 us -> none  [the longest x2 13.8 us: to_lines(): lax.all_to_all(cells, 'slab', split_axis=1, concat_axis=2, tiled=True)]
    dot_general x6 -> x4, matrix products: 7.26 us -> 2.71 us  [the longest x2 2.16 us: spread(): return jnp.dot(picked, pick_source, precision=highest)]
    reshape x0 -> x2, local copies, waits for them, and re-layouts: none -> 3.22 us  [the longest x1 1.72 us: solve(): return solved.reshape(seeded.shape)]
    dot_general x2 -> x0, local copies, waits for them, and re-layouts: 2.51 us -> none  [solve_zy(): return jnp.einsum('jk,cxzj->cxzk', inv_y, lines, precision=highest)]
    all_to_all x6 -> x0, local copies, waits for them, and re-layouts: 1.98 us -> none  [the longest x4 1.55 us: to_cells(): lax.all_to_all(lines, 'slab', split_axis=2, concat_axis=1, tiled=True)]
  transfers between devices with their start and end apart: 10 -> 4, of which waited for: 7 -> 0; matrix products, arithmetic and copies ran while one was open for 7% -> 1% of each run, Pallas kernels for 0% -> 0%
where the time goes in v2:
time: 101 us
  Pallas kernels  74.1 us (73%)
  starting transfers between devices  10.8 us (11%)
  local copies, waits for them, and re-layouts  8.4 us (8%)
  matrix products  4.36 us (4%)
  other arithmetic  2.62 us (3%)
    pallas_call x1, Pallas kernels, solve(): pl.pallas_call(functools.partial(solve_kernel, slabs, grps), out_shape=ja...  74.1 us
    ppermute x2, starting transfers between devices, neighbours(): before = lax.ppermute(tail, axis, [(i, i + 1) for i in range(ends)])  7.3 us
    ppermute x2, starting transfers between devices, neighbours(): after = lax.ppermute(head, axis, [(i + 1, i) for i in range(ends)])  3.54 us
    dot_general x2, matrix products, spread(): return jnp.dot(picked, pick_source, precision=highest)  2.16 us
  transfers between devices with their start and end apart: 4, of which 0 were waited for; matrix products, arithmetic and copies ran while one was open for 1% of the time, Pallas kernels for 0%

profile of v2, /device:TPU:1, one launch (start us, length us, event | category | flops | bytes accessed | tf_op | source)
XLA Modules:
  0.0 100.7 jit_solution(5461779166100260149)
XLA Ops:
  0.0 0.0 copy-start
  0.0 0.0 copy-start.7
  0.0 0.0 copy-start.9
  0.0 0.0 copy-start.8
  0.1 0.6 copy-done.7
  0.7 0.0 copy-done.6
  0.7 0.0 copy-done.9
  0.7 0.0 copy-done.8
  0.8 1.6 %fusion = f32[256,256]{1,0:T(8,128)S(1)} fusion(f32[2048]{0:T(1024)S(1)} %copy-done.8, s32[2048]{0:T(1024)S(1)} %copy-done.9, s32[2048]{0:T(1024)S(1)} %add_select_fusion), kind=kOutput, calls=%fused_computation | convolution fusion | flops 1612185600 | bytes 286720 | tf_op jit(solution)/shard_map/dot_general | solution.py:39
  2.4 0.1 reshape.169
  2.5 0.0 copy-done.1
  2.5 0.1 add_dynamic-update-slice_fusion
  2.6 0.0 copy-start.5
  2.6 1.5 %reshape.170.cells = f32[5,16,16,256]{3,2,1,0:T(8,128)} reshape(f32[5,64,4,256]{3,2,1,0:T(4,128)S(1)} %add_dynamic-update-slice_fusion) | data formatting | bytes 2621440 | tf_op jit(solution)/shard_map/reshape | solution.py:176
  4.1 0.0 copy-done.5
  4.1 0.3 fusion.12
  4.4 1.0 convolution_select_fusion.1.mat_z
  5.4 0.0 copy-done
  5.4 0.3 fusion.11
  5.7 1.2 %convolution_select_fusion.mat_x = f32[256,512]{1,0:T(8,128)} fusion(f32[256,128]{1,0:T(8,128)S(1)} %fusion.11, s32[512]{0:T(512)S(1)} %get-tuple-element.31, s32[256]{0:T(256)S(1)} %and_select_fusion.3, s32[512]{0:T(512)S(1)} %get-tuple-element.30), kind=kOutput, calls=%fused_computation.10 | convolution fusion | flops 201654272 | bytes 660480 | tf_op jit(solution)/shard_map/dot_general | solution.py:141
  6.9 74.1 %shard_map.109 = f32[5,16,16,256]{3,2,1,0:T(8,128)} custom-call(f32[5,16,16,256]{3,2,1,0:T(8,128)} %reshape.170.cells, f32[256,512]{1,0:T(8,128)} %convolution_select_fusion.mat_x, f32[256,256]{1,0:T(8,128)} %convolution_select_fusion.1.mat_z, f32[256,256]{1,0:T(8,128)} %mat_y.1), custom_call_target="tpu_custom_call" | custom-call | tf_op jit(solution)/shard_map/pallas_call | solution.py:160
  81.0 0.0 copy-start.3
  81.0 1.7 %reshape.171 = f32[5,64,4,256]{3,2,1,0:T(4,128)S(1)} reshape(f32[5,16,16,256]{3,2,1,0:T(8,128)} %shard_map.109) | data formatting | bytes 2621440 | tf_op jit(solution)/shard_map/reshape | solution.py:177
  82.7 0.0 copy-done.3
  82.8 0.1 copy.12
  82.8 0.3 copy_multiply_fusion
  83.2 2.2 %collective-permute-start.2 = (f32[5,64,1,256]{3,1,2,0:T(8,128)S(1)}, f32[5,64,1,256]{3,1,2,0:T(8,128)S(1)}, u32[]{:S(2)}, u32[]{:S(2)}) collective-permute-start(f32[5,64,1,256]{3,1,2,0:T(8,128)S(1)} %get-tuple-element.23), channel_id=1, source_target_pairs={{2,0},{4,2},{6,4},{8,6},{10,8},{12,10},{14,12},{16,14},{18,16},{20... | collective-permute-start | bytes 983048 | tf_op jit(solution)/shard_map/ppermute | solution.py:20
  85.4 3.3 %collective-permute-start.3 = (f32[5,64,1,256]{3,1,2,0:T(8,128)S(1)}, f32[5,64,1,256]{3,1,2,0:T(8,128)S(1)}, u32[]{:S(2)}, u32[]{:S(2)}) collective-permute-start(f32[5,64,1,256]{3,1,2,0:T(8,128)S(1)} %get-tuple-element.24), channel_id=1, source_target_pairs={{0,2},{2,4},{4,6},{6,8},{8,10},{10,12},{12,14},{14,16},{16,18},{18... | collective-permute-start | bytes 983048 | tf_op jit(solution)/shard_map/ppermute | solution.py:19
  88.8 1.3 %collective-permute-start = (f32[5,1,4,256]{3,1,2,0:T(1,128)S(1)}, f32[5,1,4,256]{3,1,2,0:T(1,128)S(1)}, u32[]{:S(2)}, u32[]{:S(2)}) collective-permute-start(f32[5,1,4,256]{3,1,2,0:T(1,128)S(1)} %get-tuple-element.19), channel_id=1, source_target_pairs={{1,0},{3,2},{5,4},{7,6},{9,8},{11,10},{13,12},{15,14},{17,16},{19,... | collective-permute-start | bytes 61448 | tf_op jit(solution)/shard_map/ppermute | solution.py:20
  90.1 4.0 %collective-permute-start.1 = (f32[5,1,4,256]{3,1,2,0:T(1,128)S(1)}, f32[5,1,4,256]{3,1,2,0:T(1,128)S(1)}, u32[]{:S(2)}, u32[]{:S(2)}) collective-permute-start(f32[5,1,4,256]{3,1,2,0:T(1,128)S(1)} %get-tuple-element.20), channel_id=1, source_target_pairs={{0,1},{2,3},{4,5},{6,7},{8,9},{10,11},{12,13},{14,15},{16,17},{18,... | collective-permute-start | bytes 61448 | tf_op jit(solution)/shard_map/ppermute | solution.py:19
  94.1 0.3 fusion.28
  94.3 0.4 fusion.32
  94.8 0.0 copy-start.2
  94.8 0.2 fusion.30
  95.0 0.8 copy-done.2
  95.8 0.1 convert_element_type.7
  95.9 0.0 copy-start.4
  95.9 0.2 fusion.8
  96.1 0.1 copy.14
  96.1 0.1 copy.15
  96.2 0.1 copy.16
  96.3 0.5 copy-done.4
  96.8 0.0 collective-permute-done
  96.8 0.0 collective-permute-done.1
  96.8 0.0 collective-permute-done.2
  96.8 0.0 collective-permute-done.3
  96.9 1.9 %multiply_add_fusion = f32[5,64,4,256]{3,1,2,0:T(8,128)S(1)} fusion(f32[5,64,4,255]{3,1,2,0:T(8,128)S(1)} %get-tuple-element.26, f32[5,64,4,255]{3,1,2,0:T(8,128)S(1)} %get-tuple-element.25, f32[5,64,3,256]{3,1,2,0:T(8,128)S(1)} %get-tuple-element.22, f32[5,64,1,256]{3,1,2,0:T(8,128)S(1)} %collective-permute-done.3, ...), kind=kLoop, calls=%fused_computation.9 | loop fusion | flops 7864320 | bytes 11786240 | tf_op jit(solution)/shard_map/add | solution.py:211
  98.8 1.9 %copy.18 = f32[5,64,4,256]{3,2,1,0:T(4,128)} copy(f32[5,64,4,256]{3,1,2,0:T(8,128)S(1)} %multiply_add_fusion) | data formatting | bytes 2621440 | tf_op jit(solution)/shard_map/add | solution.py:211
  (11 shorter events, 0.2 us)
Async XLA Ops:
  0.0 5.4 %copy-start = (f32[128,64]{0,1:T(8,128)S(1)}, f32[128,64]{0,1:T(8,128)}, u32[]{:S(2)}) copy-start(f32[128,64]{0,1:T(8,128)} %param.21) | copy-start | bytes 98308
  0.0 0.7 copy-start.7
  0.0 0.7 copy-start.6
  0.0 0.7 copy-start.9
  0.0 0.7 copy-start.8
  0.8 1.7 %copy-start.1 = (f32[5,64,4,256]{3,2,1,0:T(4,128)S(1)}, f32[5,64,4,256]{3,2,1,0:T(4,128)}, u32[]{:S(2)}) copy-start(f32[5,64,4,256]{3,2,1,0:T(4,128)} %param.13) | copy-start | bytes 3932164
  2.6 1.5 %copy-start.5 = (f32[64,64]{1,0:T(8,128)S(1)}, f32[64,64]{1,0:T(8,128)}, u32[]{:S(2)}) copy-start(f32[64,64]{1,0:T(8,128)} %param.23) | copy-start | bytes 49156
  81.0 1.7 %copy-start.3 = (s32[64,4,256]{2,1,0:T(4,128)S(1)}, s32[64,4,256]{2,1,0:T(4,128)}, u32[]{:S(2)}) copy-start(s32[64,4,256]{2,1,0:T(4,128)} %param.16) | copy-start | bytes 786436
  83.2 13.7 %collective-permute-start.2 = (f32[5,64,1,256]{3,1,2,0:T(8,128)S(1)}, f32[5,64,1,256]{3,1,2,0:T(8,128)S(1)}, u32[]{:S(2)}, u32[]{:S(2)}) collective-permute-start(f32[5,64,1,256]{3,1,2,0:T(8,128)S(1)} %get-tuple-element.23), channel_id=1, source_target_pairs={{2,0},{4,2},{6,4},{8,6},{10,8},{12,10},{14,12},{16,14},{18,16},{20... | collective-permute-start | bytes 983048 | tf_op jit(solution)/shard_map/ppermute | solution.py:20
  85.4 11.4 %collective-permute-start.3 = (f32[5,64,1,256]{3,1,2,0:T(8,128)S(1)}, f32[5,64,1,256]{3,1,2,0:T(8,128)S(1)}, u32[]{:S(2)}, u32[]{:S(2)}) collective-permute-start(f32[5,64,1,256]{3,1,2,0:T(8,128)S(1)} %get-tuple-element.24), channel_id=1, source_target_pairs={{0,2},{2,4},{4,6},{6,8},{8,10},{10,12},{12,14},{14,16},{16,18},{18... | collective-permute-start | bytes 983048 | tf_op jit(solution)/shard_map/ppermute | solution.py:19
  88.8 8.0 %collective-permute-start = (f32[5,1,4,256]{3,1,2,0:T(1,128)S(1)}, f32[5,1,4,256]{3,1,2,0:T(1,128)S(1)}, u32[]{:S(2)}, u32[]{:S(2)}) collective-permute-start(f32[5,1,4,256]{3,1,2,0:T(1,128)S(1)} %get-tuple-element.19), channel_id=1, source_target_pairs={{1,0},{3,2},{5,4},{7,6},{9,8},{11,10},{13,12},{15,14},{17,16},{19,... | collective-permute-start | bytes 61448 | tf_op jit(solution)/shard_map/ppermute | solution.py:20
  90.1 6.8 %collective-permute-start.1 = (f32[5,1,4,256]{3,1,2,0:T(1,128)S(1)}, f32[5,1,4,256]{3,1,2,0:T(1,128)S(1)}, u32[]{:S(2)}, u32[]{:S(2)}) collective-permute-start(f32[5,1,4,256]{3,1,2,0:T(1,128)S(1)} %get-tuple-element.20), channel_id=1, source_target_pairs={{0,1},{2,3},{4,5},{6,7},{8,9},{10,11},{12,13},{14,15},{16,17},{18,... | collective-permute-start | bytes 61448 | tf_op jit(solution)/shard_map/ppermute | solution.py:19
  94.8 1.0 copy-start.2
  95.9 0.9 copy-start.4

commit v3 on v2

--- a/solution.py
+++ b/solution.py
@@ -9,16 +9,6 @@
 
 time_step = 0.08
 highest = lax.Precision.HIGHEST
-
-
-def neighbours(cells, axis, dim):
-    count = lax.axis_size(axis)
-    ends = count - 1
-    head = lax.slice_in_dim(cells, 0, 1, axis=dim)
-    tail = lax.slice_in_dim(cells, cells.shape[dim] - 1, cells.shape[dim], axis=dim)
-    before = lax.ppermute(tail, axis, [(i, i + 1) for i in range(ends)])
-    after = lax.ppermute(head, axis, [(i + 1, i) for i in range(ends)])
-    return before, after
 
 
 def shifted(cells, before, after, dim):
@@ -55,9 +45,10 @@
 
 
 def solve_kernel(
-    slabs, grps, cells, mat_x, mat_z, mat_y, out,
-    xin, xdone, lines, zdone, ret,
-    x_send, x_recv, l_send, l_recv, r_send, r_recv,
+    slabs, grps, z_rows, cells, fluid, mat_x, mat_z, mat_y,
+    out, z_before, z_after, x_before, x_after,
+    xin, xdone, lines, zdone, ret, z_faces, x_faces, z_halo, x_halo,
+    x_send, x_recv, l_send, l_recv, r_send, r_recv, h_send, h_recv,
 ):
     fields = cells.shape[0]
     rows = cells.shape[1] * cells.shape[2]
@@ -119,14 +110,43 @@
 
         lax.fori_loop(1, slabs, to_slab, 0)
 
-    for c in range(fields + 2):
+    block_rows = cells.shape[2]
+    x_part = block_rows // z_rows
+
+    def halos(c):
+        return (
+            (z_faces.at[c, 0], z_halo.at[c, 0], "slab", lax.rem(me + 1, slabs)),
+            (z_faces.at[c, 1], z_halo.at[c, 1], "slab", lax.rem(me + slabs - 1, slabs)),
+            (x_faces.at[c, 0], x_halo.at[c, 0], "grp", lax.rem(mine + 1, grps)),
+            (x_faces.at[c, 1], x_halo.at[c, 1], "grp", lax.rem(mine + grps - 1, grps)),
+        )
+
+    def mask_stage(c):
+        wait_bytes(ret.at[c, pl.ds(0, slabs - 1)], r_recv.at[c])
+        out[c] = ret[c] * fluid[...]
+        for i in range(x_part):
+            z_faces[c, 0, :, pl.ds(i, 1), :] = out[c, :, pl.ds((i + 1) * z_rows - 1, 1), :]
+            z_faces[c, 1, :, pl.ds(i, 1), :] = out[c, :, pl.ds(i * z_rows, 1), :]
+        x_faces[c, 0] = out[c, slabs - 1, pl.ds(block_rows - z_rows, z_rows), :]
+        x_faces[c, 1] = out[c, 0, pl.ds(0, z_rows), :]
+        for h, (src, dst, axis, to) in enumerate(halos(c)):
+            send(src, dst, h_send.at[c, h], h_recv.at[c, h], axis, to)
+
+    for c in range(fields + 4):
         if c < fields:
             x_stage(c)
-        if c >= 2:
+        if 2 <= c < fields + 2:
             z_stage(c - 2)
+        if c >= 4:
+            mask_stage(c - 4)
     for c in range(fields):
-        wait_bytes(ret.at[c, pl.ds(0, slabs - 1)], r_recv.at[c])
-        out[c] = ret[c]
+        for h, (src, dst, _, _) in enumerate(halos(c)):
+            wait_bytes(dst, h_recv.at[c, h])
+            wait_bytes(src, h_send.at[c, h])
+        z_before[c] = z_halo[c, 0]
+        z_after[c] = z_halo[c, 1]
+        x_before[c] = x_halo[c, 0]
+        x_after[c] = x_halo[c, 1]
     for c in range(fields):
         wait_bytes(xin.at[c, pl.ds(0, grps - 1)], x_send.at[c])
         wait_bytes(lines.at[c, pl.ds(0, slabs - 1)], l_send.at[c])
@@ -141,7 +161,7 @@
     return jnp.dot(picked, pick_source, precision=highest)
 
 
-def solve(seeded, inv_x, inv_y, inv_z):
+def solve(seeded, fluid, inv_x, inv_y, inv_z):
     fields, x_rows, z_rows, width = seeded.shape
     slabs, grps = lax.axis_size("slab"), lax.axis_size("grp")
     x_part = x_rows // slabs
@@ -157,24 +177,45 @@
     mat_z = jnp.where(line_x[:, None] == line_x[None, :], mat_z, 0.0)
     whole = pl.BlockSpec(memory_space=pltpu.VMEM)
     sems = pltpu.SemaphoreType.DMA((fields,))
-    solved = pl.pallas_call(
-        functools.partial(solve_kernel, slabs, grps),
-        out_shape=jax.ShapeDtypeStruct((fields,) + block, jnp.float32),
-        in_specs=[whole] * 4,
-        out_specs=whole,
+    z_face = (slabs, x_part, width)
+    x_face = (z_rows, width)
+    shapes = [block, z_face, z_face, x_face, x_face]
+    masked, z_before, z_after, x_before, x_after = pl.pallas_call(
+        functools.partial(solve_kernel, slabs, grps, z_rows),
+        out_shape=[jax.ShapeDtypeStruct((fields,) + shape, jnp.float32) for shape in shapes],
+        in_specs=[whole] * 5,
+        out_specs=[whole] * 5,
         scratch_shapes=[
             pltpu.VMEM((fields, grps) + block, jnp.float32),
             pltpu.VMEM((fields,) + block, jnp.float32),
             pltpu.VMEM((fields,) + block, jnp.float32),
             pltpu.VMEM((fields,) + block, jnp.float32),
             pltpu.VMEM((fields,) + block, jnp.float32),
+            pltpu.VMEM((fields, 2) + z_face, jnp.float32),
+            pltpu.VMEM((fields, 2) + x_face, jnp.float32),
+            pltpu.VMEM((fields, 2) + z_face, jnp.float32),
+            pltpu.VMEM((fields, 2) + x_face, jnp.float32),
         ]
-        + [sems] * 6,
+        + [sems] * 6
+        + [pltpu.SemaphoreType.DMA((fields, 4))] * 2,
         compiler_params=pltpu.CompilerParams(
             collective_id=0, has_side_effects=True, vmem_limit_bytes=56 * 1024 * 1024
         ),
-    )(seeded.reshape((fields,) + block), mat_x, mat_z, inv_y)
-    return solved.reshape(seeded.shape)
+    )(seeded.reshape((fields,) + block), fluid.reshape(block), mat_x, mat_z, inv_y)
+    me, mine = lax.axis_index("slab"), lax.axis_index("grp")
+
+    def inner(halo, edge, shape):
+        return jnp.where(edge, 0.0, halo.reshape(shape))
+
+    z_shape = (fields, x_rows, 1, width)
+    x_shape = (fields, 1, z_rows, width)
+    return (
+        masked.reshape(seeded.shape),
+        inner(z_before, me == 0, z_shape),
+        inner(z_after, me == slabs - 1, z_shape),
+        inner(x_before, mine == 0, x_shape),
+        inner(x_after, mine == grps - 1, x_shape),
+    )
 
 
 def body(
@@ -192,11 +233,9 @@
 ):
     fields, x_rows, z_rows, y_cells = adj_out.shape
     pushed = marker_push((x_rows, z_rows, y_cells), marker_x, marker_z, marker_y, drag_weight)
-    solved = solve(adj_out.at[0].add(pushed), inv_x, inv_y, inv_z)
     fluid = body_mask.astype(jnp.float32)
-    masked = solved * fluid
-    z_before, z_after = neighbours(masked, "slab", 2)
-    x_before, x_after = neighbours(masked, "grp", 1)
+    seeded = adj_out.at[0].add(pushed)
+    masked, z_before, z_after, x_before, x_after = solve(seeded, fluid, inv_x, inv_y, inv_z)
     x_down, x_up = shifted(masked, x_before, x_after, 1)
     z_down, z_up = shifted(masked, z_before, z_after, 2)
     y_edge = jnp.zeros_like(masked[..., :1])

time: 101 us -> 102 us (level); the launches traced: 101 us -> 100 us
  starting transfers between devices: 10.8 us -> 0 us
  Pallas kernels: 74.1 us -> 81.2 us
  other arithmetic: 2.62 us -> 6.06 us
    ppermute x4 -> x0, starting transfers between devices: 10.8 us -> none  [the longest x2 7.3 us: neighbours(): before = lax.ppermute(tail, axis, [(i, i + 1) for i in range(ends)])]
    pallas_call x1, Pallas kernels: 74.1 us -> 81.2 us  [solve(): pl.pallas_call(functools.partial(solve_kernel, slabs, grps, z_rows), out_...]
    add x1, other arithmetic: 1.92 us -> 4.44 us  [body(): return masked + time_step * change]
    add x1 -> x0, local copies, waits for them, and re-layouts: 1.9 us -> none  [body(): return masked + time_step * change]
    select_n x0 -> x4, other arithmetic: none -> 1.15 us  [inner(): return jnp.where(edge, 0.0, halo.reshape(shape))]
    reshape x1 -> x2, local copies, waits for them, and re-layouts: 1.72 us -> 2.52 us  [the longest x1 1.72 us: solve(): masked.reshape(seeded.shape)]
  transfers between devices with their start and end apart: 4 -> 0, of which waited for: 0 -> 0; matrix products, arithmetic and copies ran while one was open for 1% -> 0% of each run, Pallas kernels for 0% -> 0%
where the time goes in v3:
time: 102 us; the launch traced here: 100 us
  Pallas kernels  81.2 us (80%)
  local copies, waits for them, and re-layouts  8.36 us (8%)
  other arithmetic  6.06 us (6%)
  matrix products  4.37 us (4%)
    pallas_call x1, Pallas kernels, solve(): pl.pallas_call(functools.partial(solve_kernel, slabs, grps, z_rows), out_...  81.2 us
    add x1, other arithmetic, body(): return masked + time_step * change  4.44 us
    dot_general x2, matrix products, spread(): return jnp.dot(picked, pick_source, precision=highest)  2.16 us

profile of v3, /device:TPU:1, one launch (start us, length us, event | category | flops | bytes accessed | tf_op | source)
XLA Modules:
  0.0 100.3 jit_solution(11945158523055065576)
XLA Ops:
  0.0 0.0 copy-start
  0.0 0.0 copy-start.6
  0.0 0.0 copy-start.11
  0.0 0.0 copy-start.12
  0.0 0.0 copy-start.9
  0.0 0.0 copy-start.10
  0.1 0.7 copy-done.9
  0.8 0.0 copy-done.10
  0.8 0.0 copy-done
  0.8 0.3 fusion.11
  1.1 0.0 copy-done.6
  1.1 0.3 fusion.12
  1.4 1.0 convolution_select_fusion.1.mat_z
  2.3 0.0 copy-done.11
  2.4 0.0 copy-done.12
  2.4 0.0 copy-start.5
  2.4 0.0 copy-start.4
  2.4 1.6 %fusion = f32[256,256]{1,0:T(8,128)S(1)} fusion(f32[2048]{0:T(1024)S(1)} %copy-done.11, s32[2048]{0:T(1024)S(1)} %copy-done.12, s32[2048]{0:T(1024)S(1)} %add_select_fusion), kind=kOutput, calls=%fused_computation | convolution fusion | flops 1612185600 | bytes 286720 | tf_op jit(solution)/shard_map/dot_general | solution.py:29
  4.0 0.0 copy-start.2
  4.0 0.1 reshape.207
  4.1 0.0 copy-done.5
  4.2 0.0 copy-done.4
  4.2 0.8 reshape.209.fluid
  5.0 1.2 %convolution_select_fusion.mat_x = f32[256,512]{1,0:T(8,128)} fusion(f32[256,128]{1,0:T(8,128)S(1)} %fusion.11, s32[512]{0:T(512)S(1)} %get-tuple-element.37, s32[256]{0:T(256)S(1)} %and_select_fusion.3, s32[512]{0:T(512)S(1)} %get-tuple-element.36), kind=kOutput, calls=%fused_computation.9 | convolution fusion | flops 201654272 | bytes 660480 | tf_op jit(solution)/shard_map/dot_general | solution.py:161
  6.2 0.0 copy-done.2
  6.2 0.0 copy-start.1
  6.2 0.1 convert_element_type.7
  6.3 0.2 fusion.8
  6.5 1.0 %copy-done.1 = f32[5,64,4,256]{3,2,1,0:T(4,128)S(1)} copy-done((f32[5,64,4,256]{3,2,1,0:T(4,128)S(1)}, f32[5,64,4,256]{3,2,1,0:T(4,128)}, u32[]{:S(2)}) %copy-start.1) | copy-done | bytes 1310744
  7.5 0.1 add_dynamic-update-slice_fusion
  7.6 1.5 %reshape.208.cells = f32[5,16,16,256]{3,2,1,0:T(8,128)} reshape(f32[5,64,4,256]{3,2,1,0:T(4,128)S(1)} %add_dynamic-update-slice_fusion) | data formatting | bytes 2621440 | tf_op jit(solution)/shard_map/reshape | solution.py:204
  9.1 81.2 %shard_map.109 = (f32[5,16,16,256]{3,2,1,0:T(8,128)}, f32[5,16,4,256]{3,2,1,0:T(4,128)}, f32[5,16,4,256]{3,2,1,0:T(4,128)}, f32[5,4,256]{2,1,0:T(4,128)}, f32[5,4,256]{2,1,0:T(4,128)}) custom-call(f32[5,16,16,256]{3,2,1,0:T(8,128)} %reshape.208.cells, f32[16,16,256]{2,1,0:T(8,128)} %reshape.209.fluid, f32[256,512]{1,0:T(8,128)} %convolution_select_fusion.mat_x, ...), custom_call_target="tpu_custom_call" | custom-call | tf_op jit(solution)/shard_map/pallas_call | solution.py:183
  90.3 0.0 copy-start.8
  90.3 0.0 copy-start.7
  90.3 0.0 copy-start.3
  90.3 1.7 %reshape.210 = f32[5,64,4,256]{3,2,1,0:T(4,128)S(1)} reshape(f32[5,16,16,256]{3,2,1,0:T(8,128)} %get-tuple-element.22) | data formatting | bytes 2621440 | tf_op jit(solution)/shard_map/reshape | solution.py:213
  92.1 0.0 copy-done.8
  92.1 0.0 copy-done.7
  92.1 0.0 copy-done.3
  92.1 0.1 broadcast_select_fusion.1
  92.2 0.4 select_n.178
  92.6 1.1 %broadcast_select_fusion = f32[5,16,4,256]{3,2,1,0:T(4,128)S(1)} fusion(f32[5,16,4,256]{3,2,1,0:T(4,128)} %get-tuple-element.26, pred[]{:T(512)S(6)} %eq.147), kind=kLoop, calls=%fused_computation.23 | loop fusion | flops 81920 | bytes 655361 | tf_op jit(solution)/shard_map/jit(_where)/select_n | solution.py:208
  93.7 0.4 select_n.179
  94.1 0.3 fusion.28
  94.4 0.5 fusion.29
  94.9 0.9 fusion.30
  95.8 4.4 %multiply_add_fusion = f32[5,64,4,256]{3,2,1,0:T(4,128)} fusion(f32[5,64,4,256]{3,2,1,0:T(4,128)S(1)} %reshape.210, f32[5,64,4,255]{3,2,1,0:T(4,128)S(1)} %get-tuple-element.32, f32[5,64,4,255]{3,2,1,0:T(4,128)S(1)} %get-tuple-element.31, f32[5,64,3,256]{3,2,1,0:T(4,128)S(1)} %get-tuple-element.30, f32[5,64,1,256]{3,2,1,0:T(1,128)S(1)} %select_n.179, ...), kind=kLoop, calls=%fused_computation.8 | loop fusion | flops 7536640 | bytes 11524096 | tf_op jit(solution)/shard_map/add | solution.py:250
  (9 shorter events, 0.1 us)
Async XLA Ops:
  0.0 0.8 copy-start
  0.0 1.1 %copy-start.6 = (f32[64,64]{1,0:T(8,128)S(1)}, f32[64,64]{1,0:T(8,128)}, u32[]{:S(2)}) copy-start(f32[64,64]{1,0:T(8,128)} %param.23) | copy-start | bytes 49156
  0.0 2.3 %copy-start.11 = (f32[2048]{0:T(1024)S(1)}, f32[2048]{0:T(1024)}, u32[]{:S(2)}) copy-start(f32[2048]{0:T(1024)} %param.20) | copy-start | bytes 24580
  0.0 2.3 %copy-start.12 = (s32[2048]{0:T(1024)S(1)}, s32[2048]{0:T(1024)}, u32[]{:S(2)}) copy-start(s32[2048]{0:T(1024)} %param.19) | copy-start | bytes 24580
  0.0 0.7 copy-start.9
  0.0 0.7 copy-start.10
  2.4 1.8 %copy-start.5 = (bf16[64,4,256]{2,1,0:T(4,128)(2,1)S(1)}, bf16[64,4,256]{2,1,0:T(4,128)(2,1)}, u32[]{:S(2)}) copy-start(bf16[64,4,256]{2,1,0:T(4,128)(2,1)} %param.15) | copy-start | bytes 393220
  2.4 1.8 %copy-start.4 = (s32[64,4,256]{2,1,0:T(4,128)S(1)}, s32[64,4,256]{2,1,0:T(4,128)}, u32[]{:S(2)}) copy-start(s32[64,4,256]{2,1,0:T(4,128)} %param.16) | copy-start | bytes 786436
  4.0 2.2 %copy-start.2 = (bf16[3,64,4,256]{3,2,1,0:T(4,128)(2,1)S(1)}, bf16[3,64,4,256]{3,2,1,0:T(4,128)(2,1)}, u32[]{:S(2)}) copy-start(bf16[3,64,4,256]{3,2,1,0:T(4,128)(2,1)} %param.14) | copy-start | bytes 1179652
  6.2 1.3 %copy-start.1 = (f32[5,64,4,256]{3,2,1,0:T(4,128)S(1)}, f32[5,64,4,256]{3,2,1,0:T(4,128)}, u32[]{:S(2)}) copy-start(f32[5,64,4,256]{3,2,1,0:T(4,128)} %param.13) | copy-start | bytes 3932164
  90.3 1.8 %copy-start.8 = (f32[5,4,256]{2,1,0:T(4,128)S(1)}, f32[5,4,256]{2,1,0:T(4,128)}, u32[]{:S(2)}) copy-start(f32[5,4,256]{2,1,0:T(4,128)} %get-tuple-element.23) | copy-start | bytes 61444
  90.3 1.8 %copy-start.7 = (f32[5,4,256]{2,1,0:T(4,128)S(1)}, f32[5,4,256]{2,1,0:T(4,128)}, u32[]{:S(2)}) copy-start(f32[5,4,256]{2,1,0:T(4,128)} %get-tuple-element.24) | copy-start | bytes 61444
  90.3 1.8 %copy-start.3 = (f32[5,16,4,256]{3,2,1,0:T(4,128)S(1)}, f32[5,16,4,256]{3,2,1,0:T(4,128)}, u32[]{:S(2)}) copy-start(f32[5,16,4,256]{3,2,1,0:T(4,128)} %get-tuple-element.25) | copy-start | bytes 983044

commit v4 on v3

--- a/solution.py
+++ b/solution.py
@@ -132,13 +132,13 @@
         for h, (src, dst, axis, to) in enumerate(halos(c)):
             send(src, dst, h_send.at[c, h], h_recv.at[c, h], axis, to)
 
-    for c in range(fields + 4):
+    for c in range(fields + 2):
         if c < fields:
             x_stage(c)
-        if 2 <= c < fields + 2:
+        if c >= 2:
             z_stage(c - 2)
-        if c >= 4:
-            mask_stage(c - 4)
+    for c in range(fields):
+        mask_stage(c)
     for c in range(fields):
         for h, (src, dst, _, _) in enumerate(halos(c)):
             wait_bytes(dst, h_recv.at[c, h])

time: 102 us -> 103 us (level); the launches traced: 100 us -> 103 us
  Pallas kernels: 81.2 us -> 83.7 us
    pallas_call x1, Pallas kernels: 81.2 us -> 83.7 us  [solve(): pl.pallas_call(functools.partial(solve_kernel, slabs, grps, z_rows), out_...]
where the time goes in v4:
time: 103 us
  Pallas kernels  83.7 us (81%)
  local copies, waits for them, and re-layouts  8.36 us (8%)
  other arithmetic  6.06 us (6%)
  matrix products  4.37 us (4%)
    pallas_call x1, Pallas kernels, solve(): pl.pallas_call(functools.partial(solve_kernel, slabs, grps, z_rows), out_...  83.7 us
    add x1, other arithmetic, body(): return masked + time_step * change  4.44 us
    dot_general x2, matrix products, spread(): return jnp.dot(picked, pick_source, precision=highest)  2.16 us

profile of v4, /device:TPU:1, one launch (start us, length us, event | category | flops | bytes accessed | tf_op | source)
XLA Modules:
  0.0 102.8 jit_solution(7416373779111937127)
XLA Ops:
  0.0 0.0 copy-start
  0.0 0.0 copy-start.6
  0.0 0.0 copy-start.11
  0.0 0.0 copy-start.12
  0.0 0.0 copy-start.9
  0.0 0.0 copy-start.10
  0.1 0.7 copy-done.9
  0.8 0.0 copy-done.10
  0.8 0.0 copy-done
  0.8 0.3 fusion.11
  1.1 0.0 copy-done.6
  1.1 0.3 fusion.12
  1.4 1.0 convolution_select_fusion.1.mat_z
  2.3 0.0 copy-done.11
  2.4 0.0 copy-done.12
  2.4 0.0 copy-start.5
  2.4 0.0 copy-start.4
  2.4 1.6 %fusion = f32[256,256]{1,0:T(8,128)S(1)} fusion(f32[2048]{0:T(1024)S(1)} %copy-done.11, s32[2048]{0:T(1024)S(1)} %copy-done.12, s32[2048]{0:T(1024)S(1)} %add_select_fusion), kind=kOutput, calls=%fused_computation | convolution fusion | flops 1612185600 | bytes 286720 | tf_op jit(solution)/shard_map/dot_general | solution.py:29
  4.0 0.0 copy-start.2
  4.0 0.1 reshape.207
  4.1 0.0 copy-done.5
  4.2 0.0 copy-done.4
  4.2 0.8 reshape.209.fluid
  5.0 1.2 %convolution_select_fusion.mat_x = f32[256,512]{1,0:T(8,128)} fusion(f32[256,128]{1,0:T(8,128)S(1)} %fusion.11, s32[512]{0:T(512)S(1)} %get-tuple-element.37, s32[256]{0:T(256)S(1)} %and_select_fusion.3, s32[512]{0:T(512)S(1)} %get-tuple-element.36), kind=kOutput, calls=%fused_computation.9 | convolution fusion | flops 201654272 | bytes 660480 | tf_op jit(solution)/shard_map/dot_general | solution.py:161
  6.2 0.0 copy-done.2
  6.2 0.0 copy-start.1
  6.2 0.1 convert_element_type.7
  6.3 0.2 fusion.8
  6.5 1.0 copy-done.1
  7.5 0.1 add_dynamic-update-slice_fusion
  7.6 1.5 %reshape.208.cells = f32[5,16,16,256]{3,2,1,0:T(8,128)} reshape(f32[5,64,4,256]{3,2,1,0:T(4,128)S(1)} %add_dynamic-update-slice_fusion) | data formatting | bytes 2621440 | tf_op jit(solution)/shard_map/reshape | solution.py:204
  9.1 83.7 %shard_map.109 = (f32[5,16,16,256]{3,2,1,0:T(8,128)}, f32[5,16,4,256]{3,2,1,0:T(4,128)}, f32[5,16,4,256]{3,2,1,0:T(4,128)}, f32[5,4,256]{2,1,0:T(4,128)}, f32[5,4,256]{2,1,0:T(4,128)}) custom-call(f32[5,16,16,256]{3,2,1,0:T(8,128)} %reshape.208.cells, f32[16,16,256]{2,1,0:T(8,128)} %reshape.209.fluid, f32[256,512]{1,0:T(8,128)} %convolution_select_fusion.mat_x, ...), custom_call_target="tpu_custom_call" | custom-call | tf_op jit(solution)/shard_map/pallas_call | solution.py:183
  92.8 0.0 copy-start.8
  92.8 0.0 copy-start.7
  92.8 0.0 copy-start.3
  92.8 1.7 %reshape.210 = f32[5,64,4,256]{3,2,1,0:T(4,128)S(1)} reshape(f32[5,16,16,256]{3,2,1,0:T(8,128)} %get-tuple-element.22) | data formatting | bytes 2621440 | tf_op jit(solution)/shard_map/reshape | solution.py:213
  94.6 0.0 copy-done.8
  94.6 0.0 copy-done.7
  94.6 0.0 copy-done.3
  94.6 0.1 broadcast_select_fusion.1
  94.7 0.4 select_n.178
  95.1 1.1 %broadcast_select_fusion = f32[5,16,4,256]{3,2,1,0:T(4,128)S(1)} fusion(f32[5,16,4,256]{3,2,1,0:T(4,128)} %get-tuple-element.26, pred[]{:T(512)S(6)} %eq.147), kind=kLoop, calls=%fused_computation.23 | loop fusion | flops 81920 | bytes 655361 | tf_op jit(solution)/shard_map/jit(_where)/select_n | solution.py:208
  96.2 0.4 select_n.179
  96.6 0.3 fusion.28
  96.9 0.5 fusion.29
  97.4 0.9 fusion.30
  98.3 4.4 %multiply_add_fusion = f32[5,64,4,256]{3,2,1,0:T(4,128)} fusion(f32[5,64,4,256]{3,2,1,0:T(4,128)S(1)} %reshape.210, f32[5,64,4,255]{3,2,1,0:T(4,128)S(1)} %get-tuple-element.32, f32[5,64,4,255]{3,2,1,0:T(4,128)S(1)} %get-tuple-element.31, f32[5,64,3,256]{3,2,1,0:T(4,128)S(1)} %get-tuple-element.30, f32[5,64,1,256]{3,2,1,0:T(1,128)S(1)} %select_n.179, ...), kind=kLoop, calls=%fused_computation.8 | loop fusion | flops 7536640 | bytes 11524096 | tf_op jit(solution)/shard_map/add | solution.py:250
  (9 shorter events, 0.1 us)
Async XLA Ops:
  0.0 0.8 copy-start
  0.0 1.1 %copy-start.6 = (f32[64,64]{1,0:T(8,128)S(1)}, f32[64,64]{1,0:T(8,128)}, u32[]{:S(2)}) copy-start(f32[64,64]{1,0:T(8,128)} %param.23) | copy-start | bytes 49156
  0.0 2.3 %copy-start.11 = (f32[2048]{0:T(1024)S(1)}, f32[2048]{0:T(1024)}, u32[]{:S(2)}) copy-start(f32[2048]{0:T(1024)} %param.20) | copy-start | bytes 24580
  0.0 2.3 %copy-start.12 = (s32[2048]{0:T(1024)S(1)}, s32[2048]{0:T(1024)}, u32[]{:S(2)}) copy-start(s32[2048]{0:T(1024)} %param.19) | copy-start | bytes 24580
  0.0 0.7 copy-start.9
  0.0 0.7 copy-start.10
  2.4 1.8 %copy-start.5 = (bf16[64,4,256]{2,1,0:T(4,128)(2,1)S(1)}, bf16[64,4,256]{2,1,0:T(4,128)(2,1)}, u32[]{:S(2)}) copy-start(bf16[64,4,256]{2,1,0:T(4,128)(2,1)} %param.15) | copy-start | bytes 393220
  2.4 1.8 %copy-start.4 = (s32[64,4,256]{2,1,0:T(4,128)S(1)}, s32[64,4,256]{2,1,0:T(4,128)}, u32[]{:S(2)}) copy-start(s32[64,4,256]{2,1,0:T(4,128)} %param.16) | copy-start | bytes 786436
  4.0 2.2 %copy-start.2 = (bf16[3,64,4,256]{3,2,1,0:T(4,128)(2,1)S(1)}, bf16[3,64,4,256]{3,2,1,0:T(4,128)(2,1)}, u32[]{:S(2)}) copy-start(bf16[3,64,4,256]{3,2,1,0:T(4,128)(2,1)} %param.14) | copy-start | bytes 1179652
  6.2 1.3 %copy-start.1 = (f32[5,64,4,256]{3,2,1,0:T(4,128)S(1)}, f32[5,64,4,256]{3,2,1,0:T(4,128)}, u32[]{:S(2)}) copy-start(f32[5,64,4,256]{3,2,1,0:T(4,128)} %param.13) | copy-start | bytes 3932164
  92.8 1.8 %copy-start.8 = (f32[5,4,256]{2,1,0:T(4,128)S(1)}, f32[5,4,256]{2,1,0:T(4,128)}, u32[]{:S(2)}) copy-start(f32[5,4,256]{2,1,0:T(4,128)} %get-tuple-element.23) | copy-start | bytes 61444
  92.8 1.8 %copy-start.7 = (f32[5,4,256]{2,1,0:T(4,128)S(1)}, f32[5,4,256]{2,1,0:T(4,128)}, u32[]{:S(2)}) copy-start(f32[5,4,256]{2,1,0:T(4,128)} %get-tuple-element.24) | copy-start | bytes 61444
  92.8 1.8 %copy-start.3 = (f32[5,16,4,256]{3,2,1,0:T(4,128)S(1)}, f32[5,16,4,256]{3,2,1,0:T(4,128)}, u32[]{:S(2)}) copy-start(f32[5,16,4,256]{3,2,1,0:T(4,128)} %get-tuple-element.25) | copy-start | bytes 983044

commit v5 on v2

--- a/solution.py
+++ b/solution.py
@@ -83,9 +83,9 @@
     greet("grp", mine, grps)
     pl.semaphore_wait(barrier, slabs + grps - 2)
 
-    for c in range(fields):
+    def share_x(src, c):
         def to_grp(k, carry):
-            send(cells.at[c], xin.at[c, mine], x_send.at[c], x_recv.at[c], "grp", lax.rem(mine + k, grps))
+            send(src.at[c], xin.at[c, mine], x_send.at[c], x_recv.at[c], "grp", lax.rem(mine + k, grps))
             return carry
 
         lax.fori_loop(1, grps, to_grp, 0)
@@ -93,15 +93,20 @@
     def matmul(left, right):
         return jnp.dot(left, right, precision=highest, preferred_element_type=jnp.float32)
 
+    def solve_x(src, c):
+        xin[c, mine] = src[c]
+        wait_bytes(xin.at[c, pl.ds(0, grps - 1)], x_recv.at[c])
+        return matmul(mat_x[...], xin[c].reshape(grps * rows, width)).reshape(cells.shape[1:])
+
     def x_stage(c):
-        xin[c, mine] = cells[c]
-        wait_bytes(xin.at[c, pl.ds(0, grps - 1)], x_recv.at[c])
-        xdone[c] = matmul(mat_x[...], xin[c].reshape(grps * rows, width)).reshape(cells.shape[1:])
-        lines[c, me] = xdone[c, me]
+        if c > 0:
+            xdone[c] = solve_x(cells, c)
+        ready = xdone if c > 0 else cells
+        lines[c, me] = ready[c, me]
 
         def to_slab(k, carry):
             d = lax.rem(me + k, slabs)
-            send(xdone.at[c, d], lines.at[c, me], l_send.at[c], l_recv.at[c], "slab", d)
+            send(ready.at[c, d], lines.at[c, me], l_send.at[c], l_recv.at[c], "slab", d)
             return carry
 
         lax.fori_loop(1, slabs, to_slab, 0)
@@ -119,12 +124,19 @@
 
         lax.fori_loop(1, slabs, to_slab, 0)
 
-    for c in range(fields + 2):
+    x_stage(0)
+    for c in range(1, fields):
+        share_x(cells, c)
+    for c in range(1, fields + 2):
         if c < fields:
             x_stage(c)
         if c >= 2:
             z_stage(c - 2)
-    for c in range(fields):
+        if c == fields:
+            wait_bytes(ret.at[0, pl.ds(0, slabs - 1)], r_recv.at[0])
+            share_x(ret, 0)
+    out[0] = solve_x(ret, 0)
+    for c in range(1, fields):
         wait_bytes(ret.at[c, pl.ds(0, slabs - 1)], r_recv.at[c])
         out[c] = ret[c]
     for c in range(fields):

time: 101 us -> 95.8 us (0.949)
  Pallas kernels: 74.1 us -> 68.5 us
    pallas_call x1, Pallas kernels: 74.1 us -> 68.5 us  [solve(): pl.pallas_call(functools.partial(solve_kernel, slabs, grps), out_shape=ja...]
where the time goes in v5:
time: 95.8 us; the launch traced here: 95.2 us
  Pallas kernels  68.5 us (72%)
  starting transfers between devices  11 us (11%)
  local copies, waits for them, and re-layouts  8.4 us (9%)
  matrix products  4.36 us (5%)
  other arithmetic  2.62 us (3%)
    pallas_call x1, Pallas kernels, solve(): pl.pallas_call(functools.partial(solve_kernel, slabs, grps), out_shape=ja...  68.5 us
    ppermute x2, starting transfers between devices, neighbours(): before = lax.ppermute(tail, axis, [(i, i + 1) for i in range(ends)])  7.3 us
    ppermute x2, starting transfers between devices, neighbours(): after = lax.ppermute(head, axis, [(i + 1, i) for i in range(ends)])  3.72 us
    dot_general x2, matrix products, spread(): return jnp.dot(picked, pick_source, precision=highest)  2.16 us
    unnamed x20, local copies, waits for them, and re-layouts  1.97 us
    add x1, other arithmetic, body(): return masked + time_step * change  1.92 us
  transfers between devices with their start and end apart: 4, of which 0 were waited for; matrix products, arithmetic and copies ran while one was open for 1% of the time, Pallas kernels for 0%

profile of v5, /device:TPU:1, one launch (start us, length us, event | category | flops | bytes accessed | tf_op | source)
XLA Modules:
  0.0 95.2 jit_solution(12352072559970924320)
XLA Ops:
  0.0 0.0 copy-start
  0.0 0.0 copy-start.7
  0.0 0.0 copy-start.9
  0.0 0.0 copy-start.8
  0.1 0.6 copy-done.7
  0.7 0.0 copy-done.6
  0.7 0.0 copy-done.9
  0.7 0.0 copy-done.8
  0.8 1.6 %fusion = f32[256,256]{1,0:T(8,128)S(1)} fusion(f32[2048]{0:T(1024)S(1)} %copy-done.8, s32[2048]{0:T(1024)S(1)} %copy-done.9, s32[2048]{0:T(1024)S(1)} %add_select_fusion), kind=kOutput, calls=%fused_computation | convolution fusion | flops 1612185600 | bytes 286720 | tf_op jit(solution)/shard_map/dot_general | solution.py:39
  2.4 0.1 reshape.169
  2.5 0.0 copy-done.1
  2.5 0.1 add_dynamic-update-slice_fusion
  2.6 0.0 copy-start.5
  2.6 1.5 %reshape.170.cells = f32[5,16,16,256]{3,2,1,0:T(8,128)} reshape(f32[5,64,4,256]{3,2,1,0:T(4,128)S(1)} %add_dynamic-update-slice_fusion) | data formatting | bytes 2621440 | tf_op jit(solution)/shard_map/reshape | solution.py:188
  4.1 0.0 copy-done.5
  4.1 0.3 fusion.12
  4.4 1.0 %convolution_select_fusion.1.mat_z = f32[256,256]{1,0:T(8,128)} fusion(f32[256,64]{1,0:T(8,128)S(1)} %fusion.12, s32[256]{0:T(256)S(1)} %get-tuple-element.32, s32[256]{0:T(256)S(1)} %get-tuple-element.33), kind=kOutput, calls=%fused_computation.11 | convolution fusion | flops 50479104 | bytes 329728 | tf_op jit(solution)/shard_map/dot_general | solution.py:153
  5.4 0.0 copy-done
  5.4 0.3 fusion.11
  5.7 1.2 %convolution_select_fusion.mat_x = f32[256,512]{1,0:T(8,128)} fusion(f32[256,128]{1,0:T(8,128)S(1)} %fusion.11, s32[512]{0:T(512)S(1)} %get-tuple-element.31, s32[256]{0:T(256)S(1)} %and_select_fusion.3, s32[512]{0:T(512)S(1)} %get-tuple-element.30), kind=kOutput, calls=%fused_computation.10 | convolution fusion | flops 201654272 | bytes 660480 | tf_op jit(solution)/shard_map/dot_general | solution.py:153
  6.9 68.5 %shard_map.109 = f32[5,16,16,256]{3,2,1,0:T(8,128)} custom-call(f32[5,16,16,256]{3,2,1,0:T(8,128)} %reshape.170.cells, f32[256,512]{1,0:T(8,128)} %convolution_select_fusion.mat_x, f32[256,256]{1,0:T(8,128)} %convolution_select_fusion.1.mat_z, f32[256,256]{1,0:T(8,128)} %mat_y.1), custom_call_target="tpu_custom_call" | custom-call | tf_op jit(solution)/shard_map/pallas_call | solution.py:172
  75.3 0.0 copy-start.3
  75.4 1.7 %reshape.171 = f32[5,64,4,256]{3,2,1,0:T(4,128)S(1)} reshape(f32[5,16,16,256]{3,2,1,0:T(8,128)} %shard_map.109) | data formatting | bytes 2621440 | tf_op jit(solution)/shard_map/reshape | solution.py:189
  77.1 0.0 copy-done.3
  77.2 0.1 copy.12
  77.2 0.3 copy_multiply_fusion
  77.5 2.4 %collective-permute-start.2 = (f32[5,64,1,256]{3,1,2,0:T(8,128)S(1)}, f32[5,64,1,256]{3,1,2,0:T(8,128)S(1)}, u32[]{:S(2)}, u32[]{:S(2)}) collective-permute-start(f32[5,64,1,256]{3,1,2,0:T(8,128)S(1)} %get-tuple-element.23), channel_id=1, source_target_pairs={{2,0},{4,2},{6,4},{8,6},{10,8},{12,10},{14,12},{16,14},{18,16},{20... | collective-permute-start | bytes 983048 | tf_op jit(solution)/shard_map/ppermute | solution.py:20
  80.0 3.3 %collective-permute-start.3 = (f32[5,64,1,256]{3,1,2,0:T(8,128)S(1)}, f32[5,64,1,256]{3,1,2,0:T(8,128)S(1)}, u32[]{:S(2)}, u32[]{:S(2)}) collective-permute-start(f32[5,64,1,256]{3,1,2,0:T(8,128)S(1)} %get-tuple-element.24), channel_id=1, source_target_pairs={{0,2},{2,4},{4,6},{6,8},{8,10},{10,12},{12,14},{14,16},{16,18},{18... | collective-permute-start | bytes 983048 | tf_op jit(solution)/shard_map/ppermute | solution.py:19
  83.3 1.3 %collective-permute-start = (f32[5,1,4,256]{3,1,2,0:T(1,128)S(1)}, f32[5,1,4,256]{3,1,2,0:T(1,128)S(1)}, u32[]{:S(2)}, u32[]{:S(2)}) collective-permute-start(f32[5,1,4,256]{3,1,2,0:T(1,128)S(1)} %get-tuple-element.19), channel_id=1, source_target_pairs={{1,0},{3,2},{5,4},{7,6},{9,8},{11,10},{13,12},{15,14},{17,16},{19,... | collective-permute-start | bytes 61448 | tf_op jit(solution)/shard_map/ppermute | solution.py:20
  84.6 4.0 %collective-permute-start.1 = (f32[5,1,4,256]{3,1,2,0:T(1,128)S(1)}, f32[5,1,4,256]{3,1,2,0:T(1,128)S(1)}, u32[]{:S(2)}, u32[]{:S(2)}) collective-permute-start(f32[5,1,4,256]{3,1,2,0:T(1,128)S(1)} %get-tuple-element.20), channel_id=1, source_target_pairs={{0,1},{2,3},{4,5},{6,7},{8,9},{10,11},{12,13},{14,15},{16,17},{18,... | collective-permute-start | bytes 61448 | tf_op jit(solution)/shard_map/ppermute | solution.py:19
  88.6 0.3 fusion.28
  88.9 0.4 fusion.32
  89.3 0.0 copy-start.2
  89.3 0.2 fusion.30
  89.6 0.8 copy-done.2
  90.3 0.1 convert_element_type.7
  90.4 0.0 copy-start.4
  90.4 0.2 fusion.8
  90.6 0.1 copy.14
  90.7 0.1 copy.15
  90.8 0.1 copy.16
  90.8 0.5 copy-done.4
  91.4 0.0 collective-permute-done
  91.4 0.0 collective-permute-done.1
  91.4 0.0 collective-permute-done.2
  91.4 0.0 collective-permute-done.3
  91.4 1.9 %multiply_add_fusion = f32[5,64,4,256]{3,1,2,0:T(8,128)S(1)} fusion(f32[5,64,4,255]{3,1,2,0:T(8,128)S(1)} %get-tuple-element.26, f32[5,64,4,255]{3,1,2,0:T(8,128)S(1)} %get-tuple-element.25, f32[5,64,3,256]{3,1,2,0:T(8,128)S(1)} %get-tuple-element.22, f32[5,64,1,256]{3,1,2,0:T(8,128)S(1)} %collective-permute-done.3, ...), kind=kLoop, calls=%fused_computation.9 | loop fusion | flops 7864320 | bytes 11786240 | tf_op jit(solution)/shard_map/add | solution.py:223
  93.3 1.9 %copy.18 = f32[5,64,4,256]{3,2,1,0:T(4,128)} copy(f32[5,64,4,256]{3,1,2,0:T(8,128)S(1)} %multiply_add_fusion) | data formatting | bytes 2621440 | tf_op jit(solution)/shard_map/add | solution.py:223
  (11 shorter events, 0.2 us)
Async XLA Ops:
  0.0 5.4 %copy-start = (f32[128,64]{0,1:T(8,128)S(1)}, f32[128,64]{0,1:T(8,128)}, u32[]{:S(2)}) copy-start(f32[128,64]{0,1:T(8,128)} %param.21) | copy-start | bytes 98308
  0.0 0.7 copy-start.7
  0.0 0.7 copy-start.6
  0.0 0.7 copy-start.9
  0.0 0.7 copy-start.8
  0.8 1.7 %copy-start.1 = (f32[5,64,4,256]{3,2,1,0:T(4,128)S(1)}, f32[5,64,4,256]{3,2,1,0:T(4,128)}, u32[]{:S(2)}) copy-start(f32[5,64,4,256]{3,2,1,0:T(4,128)} %param.13) | copy-start | bytes 3932164
  2.6 1.5 %copy-start.5 = (f32[64,64]{1,0:T(8,128)S(1)}, f32[64,64]{1,0:T(8,128)}, u32[]{:S(2)}) copy-start(f32[64,64]{1,0:T(8,128)} %param.23) | copy-start | bytes 49156
  75.3 1.7 %copy-start.3 = (s32[64,4,256]{2,1,0:T(4,128)S(1)}, s32[64,4,256]{2,1,0:T(4,128)}, u32[]{:S(2)}) copy-start(s32[64,4,256]{2,1,0:T(4,128)} %param.16) | copy-start | bytes 786436
  77.5 13.9 %collective-permute-start.2 = (f32[5,64,1,256]{3,1,2,0:T(8,128)S(1)}, f32[5,64,1,256]{3,1,2,0:T(8,128)S(1)}, u32[]{:S(2)}, u32[]{:S(2)}) collective-permute-start(f32[5,64,1,256]{3,1,2,0:T(8,128)S(1)} %get-tuple-element.23), channel_id=1, source_target_pairs={{2,0},{4,2},{6,4},{8,6},{10,8},{12,10},{14,12},{16,14},{18,16},{20... | collective-permute-start | bytes 983048 | tf_op jit(solution)/shard_map/ppermute | solution.py:20
  80.0 11.4 %collective-permute-start.3 = (f32[5,64,1,256]{3,1,2,0:T(8,128)S(1)}, f32[5,64,1,256]{3,1,2,0:T(8,128)S(1)}, u32[]{:S(2)}, u32[]{:S(2)}) collective-permute-start(f32[5,64,1,256]{3,1,2,0:T(8,128)S(1)} %get-tuple-element.24), channel_id=1, source_target_pairs={{0,2},{2,4},{4,6},{6,8},{8,10},{10,12},{12,14},{14,16},{16,18},{18... | collective-permute-start | bytes 983048 | tf_op jit(solution)/shard_map/ppermute | solution.py:19
  83.3 8.0 %collective-permute-start = (f32[5,1,4,256]{3,1,2,0:T(1,128)S(1)}, f32[5,1,4,256]{3,1,2,0:T(1,128)S(1)}, u32[]{:S(2)}, u32[]{:S(2)}) collective-permute-start(f32[5,1,4,256]{3,1,2,0:T(1,128)S(1)} %get-tuple-element.19), channel_id=1, source_target_pairs={{1,0},{3,2},{5,4},{7,6},{9,8},{11,10},{13,12},{15,14},{17,16},{19,... | collective-permute-start | bytes 61448 | tf_op jit(solution)/shard_map/ppermute | solution.py:20
  84.6 6.8 %collective-permute-start.1 = (f32[5,1,4,256]{3,1,2,0:T(1,128)S(1)}, f32[5,1,4,256]{3,1,2,0:T(1,128)S(1)}, u32[]{:S(2)}, u32[]{:S(2)}) collective-permute-start(f32[5,1,4,256]{3,1,2,0:T(1,128)S(1)} %get-tuple-element.20), channel_id=1, source_target_pairs={{0,1},{2,3},{4,5},{6,7},{8,9},{10,11},{12,13},{14,15},{16,17},{18,... | collective-permute-start | bytes 61448 | tf_op jit(solution)/shard_map/ppermute | solution.py:19
  89.3 1.0 %copy-start.2 = (bf16[3,64,4,256]{3,2,1,0:T(4,128)(2,1)S(1)}, bf16[3,64,4,256]{3,2,1,0:T(4,128)(2,1)}, u32[]{:S(2)}) copy-start(bf16[3,64,4,256]{3,2,1,0:T(4,128)(2,1)} %param.14) | copy-start | bytes 1179652
  90.4 0.9 copy-start.4
